TPU v7x, 256 devices: a whole 4x4x8 slice. The times are simulated.
256 devices in a mesh: tm: 32 (over y, z_hi, core), head: 8 (over z_lo, x).
Axes of the slice: x: 4, y: 4, z: 8 (z_hi: 4, z_lo: 2; z = z_hi * 2 + z_lo), core: 2. Of those that a mesh axis runs over, the one named last changes fastest.
Arguments:
- tokens: bfloat16 [8192, 3072], P('tm', 'head'), may hold values from -14 to 14
- qkv_weight: bfloat16 [3, 3072, 3072], P(None, None, 'head'), may hold values from -0.109375 to 0.109375
- out_weight: bfloat16 [3072, 3072], P('head'), may hold values from -0.109375 to 0.109375
- segment_ids: int32 [8192], replicated, may hold values from 0 to 2, never falling along the last dimension, each value on 1 to 4096 neighbouring positions
- inner_w1: float32 [48, 64, 256], P('head'), may hold values from -0.75 to 0.75
- inner_b1: float32 [48, 256], P('head'), may hold values from -3 to 3
- inner_w2: float32 [48, 256, 64], P('head'), may hold values from -0.375 to 0.375
- inner_b2: float32 [48, 64], P('head'), may hold values from -3 to 3
- norm_gain: float32 [48, 64], P('head'), may hold values from 0.1 to 1.9
- norm_bias: float32 [48, 64], P('head'), may hold values from -2 to 2
- inner_rate: float32 [48], P('head'), may hold values from 0.1 to 1
- out_gate: float32 [48, 64], P('head'), may hold values from -3 to 3
Outputs:
- layer_out: bfloat16 [8192, 3072], P('tm', 'head')
Inputs may be any that keep to these rules, and one draw needn't show every extreme that they name: `segment_ids`: segment ids never fall along the tokens; each segment has 1 to 4096 tokens and one has exactly 4096.
All inputs are finite; a program needn't handle non-finite values.
Results may differ from a plain program's by a relative error of at most 0.019.
The roundings to bfloat16 on the way count: a program that leaves them out, or rounds other values in their place, can miss the bound.
Values may be sent and summed in bfloat16 or wider, within the bound.
A program may use at most 128 MiB of HBM per device.

v0:
```python
import jax
import jax.numpy as jnp
from jax import lax
from jax.sharding import PartitionSpec as P

HDIM = 64
GROUP = 64


EPS = 1e-06
HIGH = lax.Precision.HIGHEST


def from_behind(block, axis, distance):
    devices = range(lax.axis_size(axis))
    route = [(i - distance, i) for i in devices if i - distance in devices]
    return lax.ppermute(block, axis, route)


def smooth_gate(value_in):
    return jax.nn.gelu(value_in, approximate=True)


def rms_scaled(field):
    return field * lax.rsqrt(jnp.mean(field * field, -1, keepdims=True) + EPS)


def layer_normed(field, norm_gain, norm_bias):
    center = field - jnp.mean(field, -1, keepdims=True)
    inverse = lax.rsqrt(jnp.mean(center * center, -1, keepdims=True) + EPS)
    normed = center * inverse
    return (normed, inverse, normed * norm_gain + norm_bias)


def inner_step(inner_state, pieces, head_consts):
    w_first, b_first, w_second, b_second = inner_state
    key_rows, value_rows, query_rows = pieces
    norm_gain, norm_bias, step_rate = head_consts
    hidden = jnp.dot(key_rows, w_first, precision=HIGH) + b_first
    active, gelu_back = jax.vjp(smooth_gate, hidden)
    recon = jnp.dot(active, w_second, precision=HIGH) + b_second
    normed, inverse, produced = layer_normed(recon, norm_gain, norm_bias)
    grad_norm = (produced - (value_rows - key_rows)) * norm_gain
    grad_recon = inverse * (
        grad_norm
        - jnp.mean(grad_norm, -1, keepdims=True)
        - normed * jnp.mean(grad_norm * normed, -1, keepdims=True)
    )
    grad_active = jnp.dot(grad_recon, w_second.T, precision=HIGH)
    grad_hidden = gelu_back(grad_active)[0]
    step_size = step_rate / (key_rows.shape[0] * key_rows.shape[1])
    w_first = w_first - step_size * jnp.dot(key_rows.T, grad_hidden, precision=HIGH)
    b_first = b_first - step_size * jnp.sum(grad_hidden, 0)
    w_second = w_second - step_size * jnp.dot(active.T, grad_recon, precision=HIGH)
    b_second = b_second - step_size * jnp.sum(grad_recon, 0)
    query_hidden = smooth_gate(jnp.dot(query_rows, w_first, precision=HIGH) + b_first)
    query_recon = jnp.dot(query_hidden, w_second, precision=HIGH) + b_second
    result = query_rows + layer_normed(query_recon, norm_gain, norm_bias)[2]
    return ((w_first, b_first, w_second, b_second), result)


def pack_state(inner_state):
    w_first, b_first, w_second, b_second = inner_state
    filler = jnp.zeros((w_first.shape[1] - b_second.shape[0],), jnp.float32)
    return jnp.concatenate(
        [w_first, w_second.T, b_first[None], jnp.concatenate([b_second, filler])[None]], 0
    )


def unpack_state(packed):
    depth = (packed.shape[0] - 2) // 2
    return (
        packed[:depth],
        packed[2 * depth],
        packed[depth : 2 * depth].T,
        packed[2 * depth + 1, :depth],
    )


def pass_on(packed, sign):
    return from_behind(packed, "tm", sign)


def sweep_wave(streams, init_params, consts, n_tm, place):
    heads_here = init_params[0].shape[0]

    def round_body(round_index, carry):
        updated = []
        for stream, held in zip(streams, carry):
            sign, key_rows, value_rows, query_rows = stream
            packed, outputs = held
            position = place if sign > 0 else n_tm - 1 - place
            head_slot = round_index - position
            active_flag = (head_slot >= 0) & (head_slot < heads_here)
            safe_slot = jnp.clip(head_slot, 0, heads_here - 1)

            def pick(array_in):
                return lax.dynamic_index_in_dim(array_in, safe_slot, 0, keepdims=False)

            fresh = pack_state(jax.tree.map(pick, init_params))
            start_packed = jnp.where(position == 0, fresh, packed)
            head_consts = jax.tree.map(pick, consts)

            def work(packed_in):

                def advance(carried, pieces):
                    return inner_step(carried, pieces, head_consts)

                end_state, results = lax.scan(
                    advance,
                    unpack_state(packed_in),
                    (pick(key_rows), pick(value_rows), pick(query_rows)),
                )
                return (pack_state(end_state), results)

            def resting(packed_in):
                return (packed_in, jnp.zeros(key_rows.shape[1:], jnp.float32))

            end_packed, results = lax.cond(active_flag, work, resting, start_packed)
            previous = pick(outputs)
            outputs = lax.dynamic_update_index_in_dim(
                outputs, jnp.where(active_flag, results, previous), safe_slot, 0
            )
            updated.append((pass_on(end_packed, sign), outputs))
        return tuple(updated)

    blank = jnp.zeros_like(pack_state(jax.tree.map(lambda array_in: array_in[0], init_params)))
    start = tuple(((blank, jnp.zeros(stream[1].shape, jnp.float32)) for stream in streams))
    final = lax.fori_loop(0, n_tm + heads_here - 1, round_body, start)
    return [held[1] for held in final]


def local_attention(query_flat, key_whole, value_whole, own_ids, all_ids):
    heads_here = query_flat.shape[1] // HDIM
    allowed = own_ids[:, None] == all_ids[None, :]

    def one_head(slot):
        begin = slot * HDIM
        query_tile = lax.dynamic_slice_in_dim(query_flat, begin, HDIM, 1)
        key_tile = lax.dynamic_slice_in_dim(key_whole, begin, HDIM, 1)
        value_tile = lax.dynamic_slice_in_dim(value_whole, begin, HDIM, 1)
        scores = jnp.einsum(
            "qd,kd->qk", query_tile, key_tile, preferred_element_type=jnp.float32
        ) * HDIM ** (-0.5)
        scores = jnp.where(allowed, scores, -1e30)
        top = jnp.max(scores, -1, keepdims=True)
        expo = jnp.exp(scores - top)
        total = jnp.sum(expo, -1, keepdims=True)
        weights = (expo / total).astype(jnp.bfloat16)
        return jnp.dot(weights, value_tile, preferred_element_type=jnp.float32)

    outputs = lax.map(one_head, jnp.arange(heads_here, dtype=jnp.int32))
    return jnp.transpose(outputs, (1, 0, 2))


def local(
    tokens,
    qkv_weight,
    out_weight,
    segment_ids,
    inner_w1,
    inner_b1,
    inner_w2,
    inner_b2,
    norm_gain,
    norm_bias,
    inner_rate,
    out_gate,
):
    rows = tokens.shape[0]
    heads_here = inner_w1.shape[0]
    inner_here = qkv_weight.shape[2]
    projected = jnp.einsum(
        "tw,cwf->ctf",
        lax.all_gather(tokens, "head", axis=1, tiled=True),
        qkv_weight,
        preferred_element_type=jnp.float32,
    ).astype(jnp.bfloat16)
    query_all = projected[0].reshape(rows, heads_here, HDIM)
    key_all = projected[1].reshape(rows, heads_here, HDIM)
    value_all = projected[2].reshape(rows, heads_here, HDIM)
    key_whole, value_whole = (
        lax.all_gather(projected[1], "tm", axis=0, tiled=True),
        lax.all_gather(projected[2], "tm", axis=0, tiled=True),
    )
    place = lax.axis_index("tm")
    n_tm = lax.axis_size("tm")
    own_ids = lax.dynamic_slice_in_dim(segment_ids, place * rows, rows, 0)
    attention = local_attention(projected[0], key_whole, value_whole, own_ids, segment_ids)
    count = rows // GROUP

    def to_blocks(field):
        return jnp.transpose(field.reshape(count, GROUP, heads_here, HDIM), (2, 0, 1, 3))

    def from_blocks(field):
        return jnp.transpose(field, (1, 2, 0, 3)).reshape(rows, heads_here, HDIM)

    key_rows = rms_scaled(key_all.astype(jnp.float32))
    value_rows = rms_scaled(value_all.astype(jnp.float32))
    query_rows = rms_scaled(query_all.astype(jnp.float32))
    forward_set = (1, to_blocks(key_rows), to_blocks(value_rows), to_blocks(query_rows))
    backward_set = (
        -1,
        to_blocks(key_rows[::-1]),
        to_blocks(value_rows[::-1]),
        to_blocks(query_rows[::-1]),
    )
    init_params = (inner_w1, inner_b1, inner_w2, inner_b2)
    consts = (norm_gain, norm_bias, inner_rate)
    forward_out = sweep_wave([forward_set], init_params, consts, n_tm, place)[0]
    backward_out = sweep_wave([backward_set], init_params, consts, n_tm, place)[0]
    forward = from_blocks(forward_out)
    backward = from_blocks(backward_out)[::-1]
    mixed = (
        (attention + jnp.tanh(out_gate) * (forward + backward))
        .astype(jnp.bfloat16)
        .reshape(rows, inner_here)
    )
    terms = jnp.dot(mixed, out_weight, preferred_element_type=jnp.float32)
    summed = lax.psum_scatter(terms.astype(jnp.bfloat16), "head", scatter_dimension=1, tiled=True)
    return summed


def solution(mesh):
    placed = (
        P("tm", "head"),
        P(None, None, "head"),
        P("head", None),
        P(),
        P("head", None, None),
        P("head", None),
        P("head", None, None),
        P("head", None),
        P("head", None),
        P("head", None),
        P("head"),
        P("head", None),
    )
    return jax.shard_map(
        local, mesh=mesh, in_specs=placed, out_specs=P("tm", "head"), check_vma=False
    )
```

profile of v0, /device:TPU:6, one launch (start us, length us, event | category | flops | bytes accessed | tf_op | source)
XLA Modules:
  0.0 2062.2 jit_solution(2006821102684830147)
XLA Ops:
  8.8 43.7 %all-gather.6.cloned.1.call-done = bf16[256,3072]{1,0:T(8,128)(2,1)} async-done(((bf16[256,384]{1,0:T(8,128)(2,1)}), bf16[256,3072]{1,0:T(8,128)(2,1)}) %all-gather.6.cloned.1.call-update) | async-done | bytes 1572880 | tf_op jit(solution)/shard_map/all_gather | solution.py:175
  72.8 732.6 %while.108 = (s32[]{:T(128)}, f32[130,256]{1,0:T(8,128)}, f32[6,4,64,64]{2,3,1,0:T(8,128)}, s32[]{:T(128)}, pred[]{:T(512)}, /*index=5*/f32[6,64,256]{2,1,0:T(8,...) while((s32[]{:T(128)}, f32[130,256]{1,0:T(8,128)}, ...), condition=%wide.region_20.21_spmd, body=%wide.region_7.20_spmd.sunk | while | flops 89280456 | bytes 4624120 | solution.py:129
  75.9 15.9 conditional.4
  99.4 15.9 conditional.4
  123.2 15.9 conditional.4
  150.9 15.9 conditional.4
  179.6 15.9 conditional.4
  207.4 15.9 conditional.4
  235.9 20.9 %collective-permute-start.1 = (f32[130,256]{1,0:T(8,128)S(1)}, f32[130,256]{1,0:T(8,128)S(1)}, u32[]{:S(2)}, u32[]{:S(2)}) collective-permute-start(f32[130,256]{1,0:T(8,128)S(1)} %get-tuple-element.1755), channel_id=1, source_target_pairs={{0,8},{8,16},{16,24},{24,32},{32,40},{40,48},{48,56},{56,64},{64,7... | collective-permute-start | bytes 399368 | tf_op jit(solution)/shard_map/while/body/eval_jaxpr/ppermute | solution.py:17
  275.4 21.2 %collective-permute-start.1 = (f32[130,256]{1,0:T(8,128)S(1)}, f32[130,256]{1,0:T(8,128)S(1)}, u32[]{:S(2)}, u32[]{:S(2)}) collective-permute-start(f32[130,256]{1,0:T(8,128)S(1)} %get-tuple-element.1755), channel_id=1, source_target_pairs={{0,8},{8,16},{16,24},{24,32},{32,40},{40,48},{48,56},{56,64},{64,7... | collective-permute-start | bytes 399368 | tf_op jit(solution)/shard_map/while/body/eval_jaxpr/ppermute | solution.py:17
  316.7 16.0 collective-permute-start.1
  352.6 22.5 %collective-permute-start.1 = (f32[130,256]{1,0:T(8,128)S(1)}, f32[130,256]{1,0:T(8,128)S(1)}, u32[]{:S(2)}, u32[]{:S(2)}) collective-permute-start(f32[130,256]{1,0:T(8,128)S(1)} %get-tuple-element.1755), channel_id=1, source_target_pairs={{0,8},{8,16},{16,24},{24,32},{32,40},{40,48},{48,56},{56,64},{64,7... | collective-permute-start | bytes 399368 | tf_op jit(solution)/shard_map/while/body/eval_jaxpr/ppermute | solution.py:17
  427.6 17.2 collective-permute-start.1
  499.4 20.1 collective-permute-start.1
  575.0 17.2 collective-permute-start.1
  644.9 16.7 collective-permute-start.1
  715.8 15.5 collective-permute-start.1
  785.5 17.6 collective-permute-start.1
  823.8 1132.0 %while.109 = (s32[]{:T(128)}, f32[130,256]{1,0:T(8,128)S(1)}, f32[6,4,64,64]{2,3,1,0:T(8,128)}, s32[]{:T(128)}, pred[]{:T(512)}, /*index=5*/f32[6,64,256]{2,1,0:...) while((s32[]{:T(128)}, f32[130,256]{1,0:T(8,128)S(1)}, ...), condition=%wide.region_34.35_spmd, body=%wide.region_21.34_spmd.sunk | while | flops 89280456 | bytes 4091612 | solution.py:129
  937.8 15.2 collective-permute-done
  1065.7 18.4 collective-permute-done
  1111.8 15.8 collective-permute-done
  1207.5 16.6 collective-permute-done
  1320.9 469.2 %collective-permute-done = f32[130,256]{1,0:T(8,128)S(1)} collective-permute-done((f32[130,256]{1,0:T(8,128)S(1)}, f32[130,256]{1,0:T(8,128)S(1)}, u32[]{:S(2)}, u32[]{:S(2)}) %collective-permute-start) | collective-permute-done | bytes 133152 | tf_op jit(solution)/shard_map/while/body/eval_jaxpr/ppermute | solution.py:17
  1793.3 16.0 conditional.5
  1821.8 16.0 conditional.5
  1850.2 16.0 conditional.5
  1878.9 16.0 conditional.5
  1907.4 16.0 conditional.5
  1935.9 16.0 conditional.5
  1959.9 53.3 %while.110 = (s32[]{:T(128)}, f32[6,256,64]{1,2,0:T(8,128)}, s32[6]{0:T(128)S(1)}, bf16[256,384]{0,1:T(8,128)(2,1)}, bf16[8192,384]{0,1:T(8,128)(2,1)}, /*index=...) while((s32[]{:T(128)}, f32[6,256,64]{1,2,0:T(8,128)}, ...), condition=%wide.region_3.4_spmd.clone, body=%wide.region_0.3_spmd.clone.sunk | while | flops 555744768 | bytes 27401908 | solution.py:152
  2019.1 34.8 %reduce-scatter.4.cloned.1.call-done = bf16[384,256]{1,0:T(8,128)(2,1)} async-done(((bf16[3072,256]{1,0:T(8,128)(2,1)}), bf16[384,256]{1,0:T(8,128)(2,1)}) %reduce-scatter.4.cloned.1.call-update) | async-done | bytes 196624
  (2060 shorter events, 1411.3 us)
Async XLA Ops:
  6.5 45.9 %all-gather.6.cloned.1.call-start = ((), (), s32[]{:S(2)}) async-start(), calls=%async_computation.1 | async-start | bytes 1769472 | tf_op jit(solution)/shard_map/all_gather | solution.py:175
  7.3 1952.6 %all-gather.8.cloned.1.call-start = ((), (), s32[]{:S(2)}) async-start(), calls=%async_computation.2 | async-start | bytes 6488064 | tf_op jit(solution)/shard_map/all_gather | solution.py:183
  66.1 1893.7 %all-gather.10.cloned.1.call-start = ((), (), s32[]{:S(2)}) async-start(), calls=%async_computation.3 | async-start | bytes 6488064 | tf_op jit(solution)/shard_map/all_gather | solution.py:184
  235.9 22.5 %collective-permute-start.1 = (f32[130,256]{1,0:T(8,128)S(1)}, f32[130,256]{1,0:T(8,128)S(1)}, u32[]{:S(2)}, u32[]{:S(2)}) collective-permute-start(f32[130,256]{1,0:T(8,128)S(1)} %get-tuple-element.1755), channel_id=1, source_target_pairs={{0,8},{8,16},{16,24},{24,32},{32,40},{40,48},{48,56},{56,64},{64,7... | collective-permute-start | bytes 399368 | tf_op jit(solution)/shard_map/while/body/eval_jaxpr/ppermute | solution.py:17
  275.4 22.9 %collective-permute-start.1 = (f32[130,256]{1,0:T(8,128)S(1)}, f32[130,256]{1,0:T(8,128)S(1)}, u32[]{:S(2)}, u32[]{:S(2)}) collective-permute-start(f32[130,256]{1,0:T(8,128)S(1)} %get-tuple-element.1755), channel_id=1, source_target_pairs={{0,8},{8,16},{16,24},{24,32},{32,40},{40,48},{48,56},{56,64},{64,7... | collective-permute-start | bytes 399368 | tf_op jit(solution)/shard_map/while/body/eval_jaxpr/ppermute | solution.py:17
  316.7 17.7 collective-permute-start.1
  352.6 24.1 %collective-permute-start.1 = (f32[130,256]{1,0:T(8,128)S(1)}, f32[130,256]{1,0:T(8,128)S(1)}, u32[]{:S(2)}, u32[]{:S(2)}) collective-permute-start(f32[130,256]{1,0:T(8,128)S(1)} %get-tuple-element.1755), channel_id=1, source_target_pairs={{0,8},{8,16},{16,24},{24,32},{32,40},{40,48},{48,56},{56,64},{64,7... | collective-permute-start | bytes 399368 | tf_op jit(solution)/shard_map/while/body/eval_jaxpr/ppermute | solution.py:17
  394.9 14.4 collective-permute-start.1
  427.6 18.8 collective-permute-start.1
  466.1 13.6 collective-permute-start.1
  499.4 21.8 %collective-permute-start.1 = (f32[130,256]{1,0:T(8,128)S(1)}, f32[130,256]{1,0:T(8,128)S(1)}, u32[]{:S(2)}, u32[]{:S(2)}) collective-permute-start(f32[130,256]{1,0:T(8,128)S(1)} %get-tuple-element.1755), channel_id=1, source_target_pairs={{0,8},{8,16},{16,24},{24,32},{32,40},{40,48},{48,56},{56,64},{64,7... | collective-permute-start | bytes 399368 | tf_op jit(solution)/shard_map/while/body/eval_jaxpr/ppermute | solution.py:17
  540.3 16.4 collective-permute-start.1
  575.0 18.8 collective-permute-start.1
  644.9 18.4 collective-permute-start.1
  682.4 15.2 collective-permute-start.1
  715.8 17.2 collective-permute-start.1
  752.1 15.2 collective-permute-start.1
  785.5 19.3 collective-permute-start.1
  822.5 1231.4 %reduce-scatter.4.cloned.1.call-start = ((), (), s32[]{:S(2)}) async-start(), calls=%async_computation.4 | async-start | bytes 1769472
  840.0 15.1 collective-permute-start
  874.2 15.0 collective-permute-start
  934.9 18.1 collective-permute-start
  969.5 14.3 collective-permute-start
  1000.3 16.1 collective-permute-start
  1032.8 13.6 collective-permute-start
  1062.8 21.3 %collective-permute-start = (f32[130,256]{1,0:T(8,128)S(1)}, f32[130,256]{1,0:T(8,128)S(1)}, u32[]{:S(2)}, u32[]{:S(2)}) collective-permute-start(f32[130,256]{1,0:T(8,128)S(1)} %get-tuple-element.1772), channel_id=1, source_target_pairs={{8,0},{16,8},{24,16},{32,24},{40,32},{48,40},{56,48},{64,56},{72,6... | collective-permute-start | bytes 399368 | tf_op jit(solution)/shard_map/while/body/eval_jaxpr/ppermute | solution.py:17
  1087.9 17.2 collective-permute-start
  1108.9 18.7 collective-permute-start
  1146.6 15.1 collective-permute-start
  1204.6 19.5 collective-permute-start
  1285.1 13.2 collective-permute-start
  1318.0 472.1 %collective-permute-start = (f32[130,256]{1,0:T(8,128)S(1)}, f32[130,256]{1,0:T(8,128)S(1)}, u32[]{:S(2)}, u32[]{:S(2)}) collective-permute-start(f32[130,256]{1,0:T(8,128)S(1)} %get-tuple-element.1772), channel_id=1, source_target_pairs={{8,0},{16,8},{24,16},{32,24},{40,32},{48,40},{56,48},{64,56},{72,6... | collective-permute-start | bytes 399368 | tf_op jit(solution)/shard_map/while/body/eval_jaxpr/ppermute | solution.py:17
  (90 other events, 3694.2 us)
Sparse Core Ops, SparseCore 0:
  9.2 43.2 all-gather.5
  66.2 82.7 all-gather.7
  822.7 300.8 all-gather.9
  2019.2 34.6 reduce-scatter.3
where the time goes:
time: 2080 us; the launch traced here: 2060 us
  waiting for transfers between devices  867 us (42%)
  starting transfers between devices  460 us (22%)
  local copies, waits for them, and re-layouts  446 us (21%)
  other arithmetic  131 us (6%)
  matrix products  129 us (6%)
    ppermute x74, waiting for transfers between devices, from_behind(): return lax.ppermute(block, axis, route)  787 us
    ppermute x74, starting transfers between devices, from_behind(): return lax.ppermute(block, axis, route)  459 us
    squeeze x184, local copies, waits for them, and re-layouts, pick(): return lax.dynamic_index_in_dim(array_in, safe_slot, 0, keepdims=False)  145 us
    dynamic_slice x160, local copies, waits for them, and re-layouts, pick(): return lax.dynamic_index_in_dim(array_in, safe_slot, 0, keepdims=False)  135 us
    transpose x74, local copies, waits for them, and re-layouts, pack_state(): return jnp.concatenate([w_first, w_second.T, b_first[None], jnp.concatena...  62.5 us
    dynamic_update_slice x74, other arithmetic, round_body(): lax.dynamic_update_index_in_dim(outputs, jnp.where(active_flag, results,...  61.5 us
    another operation x66, local copies, waits for them, and re-layouts  43.7 us
    all_gather x1, waiting for transfers between devices, local(): lax.all_gather(tokens, 'head', axis=1, tiled=True)  43.7 us
  transfers between devices with their start and end apart: 78, of which 38 were waited for; matrix products, arithmetic and copies ran while one was open for 30% of the time, Pallas kernels for 0%

commit v1 on v0

v1 whole, which is shorter than its diff:
```python
import functools

import jax
import jax.numpy as jnp
from jax import lax
from jax.experimental import pallas as pl
from jax.experimental.pallas import tpu as pltpu
from jax.sharding import PartitionSpec as P

MESH = pl.DeviceIdType.MESH
F = jnp.float32
B = jnp.bfloat16
HDIM = 64
GROUP = 64
EPS = 1e-06
NN = (((1,), (0,)), ((), ()))
NT = (((1,), (1,)), ((), ()))
TN = (((0,), (0,)), ((), ()))
C0 = 0.7978845608028654
C1 = 0.044715
N_TM = 32
HEADS = 6
BLOCKS = 128
PACK = 384
KEYS = 1024
CHAINS = 2 * HEADS
PER_HEAD = 3
ROLES = CHAINS + PER_HEAD * HEADS


def mm(a, b, dims=NN):
    return lax.dot_general(a, b, dims, preferred_element_type=F)


def gelu_both(x):
    x2 = x * x
    th = jnp.tanh(x * (C0 + (C0 * C1) * x2))
    hp = 0.5 + 0.5 * th
    return x * hp, hp + (hp - hp * hp) * (x * (2 * C0 + (6 * C0 * C1) * x2))


def gelu(x):
    x2 = x * x
    th = jnp.tanh(x * (C0 + (C0 * C1) * x2))
    return x * (0.5 + 0.5 * th)


def mean(x):
    return jnp.mean(x, -1, keepdims=True)


def lanes(shape):
    return lax.broadcasted_iota(jnp.int32, shape, 1)


def chain(rev, rate, buf, w1i, w2i, b2i, gain, bias, out, W1, W2, W2b, b2):
    gn, bs = gain[...], bias[...]
    g2 = gn * gn
    s = rate / (GROUP * HDIM)
    lane = lanes((64, 128))
    tail = jnp.where(lane == 64, 1.0, 0.0).astype(B)

    def place(step):
        b = jnp.clip(step, 0, BLOCKS - 1)
        b = jnp.where(rev, BLOCKS - 1 - b, b)
        return b // 4, b % 4

    def load_ka(step):
        i, j = place(step)
        return buf[i, pl.ds(pl.multiple_of(j * 64, 64), 64), :]

    def load_q(step):
        i, j = place(step)
        both = buf[i, pl.ds(pl.multiple_of(256 + (j // 2) * 64, 64), 64), :]
        swapped = jnp.concatenate([both[:, 64:], both[:, :64]], 1)
        return jnp.where(lane < 64, jnp.where(j % 2 == 0, both, swapped), tail)

    def augment(ka):
        return jnp.where(lane < 64, ka, tail)

    W1[...] = w1i[...]
    w2 = w2i[...]
    W2[...] = w2 - jnp.mean(w2, 0, keepdims=True)
    W2b[...] = W2[...].astype(B)
    start_b2 = b2i[...]
    b2[...] = start_b2 - mean(start_b2)
    first = augment(load_ka(0))
    base0 = mm(first, W1[...].astype(B))

    def body(t, carry):
        G1, base, Pt, KTs, Kt, Zlast = carry
        A = load_ka(t)[:, 64:].astype(F)
        mA = mean(A)
        W2t = W2b[...]
        b2t = b2[...]
        AW = mm(A.astype(B), W2t)
        R = mm(jnp.concatenate([Pt, KTs], 0), G1)
        Z1 = base - R[:64]
        W1n = W1[...] - R[64:]
        W1[...] = W1n
        W1b = W1n.astype(B)
        X2, dX = gelu_both(Z1)
        X2b = X2.astype(B)
        Z = mm(X2b, W2t, NT) + b2t
        Zg = Z * g2
        D = mm(jnp.concatenate([Zg.astype(B), Z.astype(B)], 0), W2t)
        S1, S2, S3, S4 = mean(Z * Z), mean(Zg), mean(Z * Zg), mean(A * Z)
        inv = lax.rsqrt(S1 + EPS)
        a1 = inv * inv
        a3 = a1 * (a1 * S3 + inv * S4)
        G1n = ((a1 * D[:64] + inv * AW - a3 * D[64:]) * dX).astype(B)
        G2 = a1 * Zg + inv * A - a3 * Z - inv * (inv * S2 + mA)
        U = mm(G2.astype(B), X2b, TN)
        W2n = W2[...] - s * U
        W2b[...] = W2n.astype(B)
        W2[...] = W2n - jnp.mean(W2n, 0, keepdims=True)
        b2n = b2t - s * jnp.sum(G2, 0, keepdims=True)
        b2[...] = b2n - mean(b2n)
        Kn = augment(load_ka(t + 1))
        Y = mm(jnp.concatenate([load_q(t - 1), Kn], 0), W1b)
        Zq = mm(gelu(Y[:64]).astype(B), W2t, NT) + b2t
        Pn = (s * mm(Kn, Kt, NT)).astype(B)
        KTn = (s * Kt.astype(F)).T.astype(B)
        z = Zlast - mean(Zlast)
        o = (z * lax.rsqrt(mean(z * z) + EPS) * gn + bs).astype(B)
        i, j = place(t - 2)
        rows = pl.ds(pl.multiple_of((j // 2) * 64, 64), 64)
        twice = jnp.concatenate([o, o], 1)
        out[i, rows, :] = jnp.where((lane < 64) == (j % 2 == 0), twice, out[i, rows, :])
        return G1n, Y[64:], Pn, KTn, Kn, Zq

    lax.fori_loop(
        0,
        BLOCKS + 2,
        body,
        (
            jnp.zeros((64, 256), B),
            base0,
            jnp.zeros((64, 64), B),
            jnp.zeros((128, 64), B),
            first,
            jnp.zeros((64, 64), F),
        ),
    )


def attend(third, c1, c2, buf, out):
    begin = (third * N_TM + PER_HEAD - 1) // PER_HEAD
    end = ((third + 1) * N_TM + PER_HEAD - 1) // PER_HEAD
    lane = lanes((128, 128))
    low = lane < 64
    per = KEYS // 256
    ones = jnp.ones((KEYS, 128), B)

    def segment(pos):
        return jnp.where(pos >= c1, 1, 0) + jnp.where(pos >= c2, 1, 0)

    row = lax.broadcasted_iota(jnp.int32, (256, 1), 0)
    inside = (row % 128) // 64 * 128 + (row // 128) * 64 + row % 64

    def block(i, _):
        both = buf[i, 256:PACK, :]
        swapped = jnp.concatenate([both[:, 64:], both[:, :64]], 1)
        zero = jnp.zeros_like(both)
        q = jnp.concatenate([jnp.where(low, both, zero), jnp.where(low, swapped, zero)], 0)
        own = segment(i * 256 + inside)

        def keys(n, carry):
            top, acc = carry
            kv = jnp.concatenate([buf[n * per + m, 0:256, :] for m in range(per)], 0)
            scores = mm(q, kv, NT)
            ids = segment(n * KEYS + lanes((1, KEYS)))
            scores = jnp.where(own == ids, scores, -1e30)
            top_new = jnp.maximum(top, jnp.max(scores, -1, keepdims=True))
            w = jnp.exp(scores - top_new).astype(B)
            fresh = mm(w, jnp.concatenate([kv, ones], 1))
            return top_new, acc * jnp.exp(top - top_new) + fresh

        start = (jnp.full((256, 1), -1e30, F), jnp.zeros((256, 256), F))
        acc = lax.fori_loop(0, N_TM * 256 // KEYS, keys, start)[1]
        o = acc[:, :128] / acc[:, 128:]
        lo = jnp.concatenate([o[:128, 64:], o[:128, :64]], 1)
        out[i] = jnp.where(low, lo, o[128:]).astype(B)
        return 0

    lax.fori_loop(begin, end, block, 0)


def role_kernel(cut_ref, rate_ref, buf, w1, w2, b2i, gain, bias, out, W1, W2, W2b, b2):
    me = lax.axis_index("tm")

    @pl.when(me < CHAINS)
    def _():
        chain(me % 2 == 1, rate_ref[0], buf, w1, w2, b2i, gain, bias, out, W1, W2, W2b, b2)

    @pl.when((me >= CHAINS) & (me < ROLES))
    def _():
        attend((me - CHAINS) % PER_HEAD, cut_ref[0], cut_ref[1], buf, out)


def greet():
    me = lax.axis_index("tm")
    barrier = pltpu.get_barrier_semaphore()

    @pl.loop(1, N_TM)
    def _(k):
        pl.semaphore_signal(
            barrier, inc=1, device_id={"tm": lax.rem(me + k, N_TM)}, device_id_type=MESH
        )

    pl.semaphore_wait(barrier, N_TM - 1)
    return me


def spread_kernel(src, buf, send_sem, recv_sem, own_sem):
    me = greet()

    def slot(d):
        return jnp.where(d < CHAINS, d // 2, HEADS + (d - CHAINS) // PER_HEAD)

    @pl.loop(1, N_TM)
    def _(k):
        d = lax.rem(me + k, N_TM)

        @pl.when(d < ROLES)
        def _():
            pltpu.make_async_remote_copy(
                src_ref=src.at[slot(d)],
                dst_ref=buf.at[me],
                send_sem=send_sem,
                recv_sem=recv_sem,
                device_id={"tm": d},
                device_id_type=MESH,
            ).start()

    @pl.when(me < ROLES)
    def _():
        own = pltpu.make_async_copy(src.at[slot(me)], buf.at[me], own_sem)
        own.start()
        own.wait()
        rest = pl.ds(0, N_TM - 1)
        pltpu.make_async_copy(buf.at[rest], buf.at[rest], recv_sem).wait()
        sent = pl.ds(0, ROLES - 1)
        pltpu.make_async_copy(buf.at[sent], buf.at[sent], send_sem).wait()

    @pl.when(me >= ROLES)
    def _():
        sent = pl.ds(0, ROLES)
        pltpu.make_async_copy(buf.at[sent], buf.at[sent], send_sem).wait()


def gather_kernel(src, res, send_sem, recv_sem, own_sem):
    me = greet()
    total = 3 * HEADS
    is_chain = me < CHAINS
    third = (me - CHAINS) % PER_HEAD
    begin = jnp.where(is_chain, 0, (third * N_TM + PER_HEAD - 1) // PER_HEAD)
    end = jnp.where(is_chain, N_TM, ((third + 1) * N_TM + PER_HEAD - 1) // PER_HEAD)
    end = jnp.where(me < ROLES, end, begin)
    slot = jnp.where(is_chain, me, CHAINS + (me - CHAINS) // PER_HEAD)
    has_own = (me >= begin) & (me < end)

    @pl.loop(0, N_TM)
    def _(i):
        @pl.when((i >= begin) & (i < end) & (i != me))
        def _():
            pltpu.make_async_remote_copy(
                src_ref=src.at[i],
                dst_ref=res.at[slot],
                send_sem=send_sem,
                recv_sem=recv_sem,
                device_id={"tm": i},
                device_id_type=MESH,
            ).start()

    @pl.when(has_own)
    def _():
        own = pltpu.make_async_copy(src.at[me], res.at[slot], own_sem)
        own.start()
        own.wait()
        rest = pl.ds(0, total - 1)
        pltpu.make_async_copy(res.at[rest], res.at[rest], recv_sem).wait()

    @pl.when(jnp.logical_not(has_own))
    def _():
        pltpu.make_async_copy(res, res, recv_sem).wait()

    count = end - begin - jnp.where(has_own, 1, 0)
    third_size = N_TM // PER_HEAD
    for amount in (third_size - 1, third_size, third_size + 1, N_TM - 1):

        @pl.when(count == amount)
        def _():
            sent = pl.ds(0, amount)
            pltpu.make_async_copy(src.at[sent], src.at[sent], send_sem).wait()


def exchange(kernel, src, shape, name, collective_id):
    return pl.pallas_call(
        kernel,
        out_shape=jax.ShapeDtypeStruct(shape, B),
        in_specs=[pl.BlockSpec(memory_space=pl.ANY)],
        out_specs=pl.BlockSpec(memory_space=pl.ANY),
        scratch_shapes=[pltpu.SemaphoreType.DMA] * 3,
        compiler_params=pltpu.CompilerParams(collective_id=collective_id, has_side_effects=True),
        name=name,
    )(src)


def rms_scaled(field):
    return field * lax.rsqrt(jnp.mean(field * field, -1, keepdims=True) + EPS)


def pair_up(field):
    heads = field.shape[0]
    split = field.reshape(heads, 2, 2, 64, 64)
    return jnp.transpose(split, (0, 1, 3, 2, 4)).reshape(heads, 128, 128)


def unpair(packed):
    count = packed.shape[0]
    split = packed.reshape(count, 2, 64, 2, 64)
    return jnp.transpose(split, (0, 1, 3, 2, 4)).reshape(count, 256, 64)


def run_roles(buf, cut, rate, w1, w2, b2, gain, bias):
    sm = pl.BlockSpec(memory_space=pltpu.SMEM)
    vm = pl.BlockSpec(memory_space=pltpu.VMEM)
    return pl.pallas_call(
        role_kernel,
        out_shape=jax.ShapeDtypeStruct((N_TM, 128, 128), B),
        in_specs=[sm, sm] + [vm] * 6,
        out_specs=vm,
        scratch_shapes=[
            pltpu.VMEM((128, 256), F),
            pltpu.VMEM((64, 256), F),
            pltpu.VMEM((64, 256), B),
            pltpu.VMEM((1, 64), F),
        ],
        compiler_params=pltpu.CompilerParams(vmem_limit_bytes=48 * 2**20),
        name="roles",
    )(cut, rate, buf, w1, w2, b2, gain, bias)


def local(
    tokens,
    qkv_weight,
    out_weight,
    segment_ids,
    inner_w1,
    inner_b1,
    inner_w2,
    inner_b2,
    norm_gain,
    norm_bias,
    inner_rate,
    out_gate,
):
    rows = tokens.shape[0]
    heads = inner_w1.shape[0]
    me = lax.axis_index("tm")
    projected = jnp.einsum(
        "tw,cwf->ctf",
        lax.all_gather(tokens, "head", axis=1, tiled=True),
        qkv_weight,
        preferred_element_type=F,
    ).astype(B)
    by_head = jnp.transpose(projected.reshape(3, rows, heads, HDIM), (0, 2, 1, 3))
    query, key, value = by_head[0], by_head[1], by_head[2]
    query_rows = rms_scaled(query.astype(F))
    key_rows = rms_scaled(key.astype(F))
    value_rows = rms_scaled(value.astype(F))
    aim = (norm_bias[:, None] - (value_rows - key_rows)) * norm_gain[:, None]
    for_chain = jnp.concatenate(
        [
            jnp.concatenate([key_rows.astype(B), aim.astype(B)], 2),
            pair_up(query_rows.astype(B)),
        ],
        1,
    )
    for_attention = jnp.concatenate(
        [jnp.concatenate([key, value], 2), pair_up(query * jnp.asarray(HDIM**-0.5, B))], 1
    )
    buf = exchange(
        spread_kernel,
        jnp.concatenate([for_chain, for_attention], 0),
        (N_TM, PACK, 128),
        "spread",
        1,
    )
    head = jnp.where(me < CHAINS, me // 2, 0)

    def pick(array):
        return lax.dynamic_index_in_dim(array, head, 0, keepdims=False)

    w1 = jnp.concatenate([pick(inner_w1), pick(inner_b1)[None], jnp.zeros((63, 256), F)], 0)
    cut = jnp.stack([jnp.sum(segment_ids < 1), jnp.sum(segment_ids < 2)]).astype(jnp.int32)
    done = run_roles(
        buf,
        cut,
        pick(inner_rate).reshape(1),
        w1,
        pick(inner_w2).T,
        pick(inner_b2)[None],
        pick(norm_gain)[None],
        pick(norm_bias)[None],
    )
    res = unpair(exchange(gather_kernel, done, (3 * HEADS, 128, 128), "collect", 2)).astype(F)
    sweeps = res[:CHAINS].reshape(heads, 2, rows, HDIM)
    swept = sweeps[:, 0] + sweeps[:, 1] + 2.0 * query_rows
    mixed = (res[CHAINS:] + jnp.tanh(out_gate)[:, None] * swept).astype(B)
    mixed = jnp.transpose(mixed, (1, 0, 2)).reshape(rows, heads * HDIM)
    terms = jnp.dot(mixed, out_weight, preferred_element_type=F)
    return lax.psum_scatter(terms.astype(B), "head", scatter_dimension=1, tiled=True)


def solution(mesh):
    placed = (
        P("tm", "head"),
        P(None, None, "head"),
        P("head", None),
        P(),
        P("head", None, None),
        P("head", None),
        P("head", None, None),
        P("head", None),
        P("head", None),
        P("head", None),
        P("head"),
        P("head", None),
    )
    return jax.shard_map(
        local, mesh=mesh, in_specs=placed, out_specs=P("tm", "head"), check_vma=False
    )
```

time: 2080 us -> 384 us (0.18)
  waiting for transfers between devices: 867 us -> 80.5 us
  starting transfers between devices: 460 us -> 0.04 us
  local copies, waits for them, and re-layouts: 446 us -> 45.1 us
  Pallas kernels: 0 us -> 219 us
  matrix products: 129 us -> 7.73 us
  other arithmetic: 131 us -> 14.7 us
    ppermute x74 -> x0, waiting for transfers between devices: 787 us -> none  [from_behind(): return lax.ppermute(block, axis, route)]
    ppermute x74 -> x0, starting transfers between devices: 459 us -> none  [from_behind(): return lax.ppermute(block, axis, route)]
    pallas_call x0 -> x3, Pallas kernels: none -> 219 us  [the longest x1 115 us: run_roles(): pl.pallas_call(role_kernel, out_shape=jax.ShapeDtypeStruct((N_TM, 128, 12...]
    squeeze x196 -> x1, local copies, waits for them, and re-layouts: 145 us -> 0.84 us  [pick(): return lax.dynamic_index_in_dim(array, head, 0, keepdims=False)]
    dynamic_slice x167 -> x4, local copies, waits for them, and re-layouts: 139 us -> 3.34 us  [pick(): return lax.dynamic_index_in_dim(array, head, 0, keepdims=False)]
    dot_general x349 -> x1, matrix products: 124 us -> 2.16 us  [local(): terms = jnp.dot(mixed, out_weight, preferred_element_type=F)]
    dynamic_update_slice x122 -> x0, other arithmetic: 95 us -> none  [the longest x74 61.5 us: round_body(): lax.dynamic_update_index_in_dim(outputs, jnp.where(active_flag, results,...]
    transpose x88 -> x3, local copies, waits for them, and re-layouts: 66.8 us -> 2.18 us  [the longest x1 1.17 us: pair_up(): return jnp.transpose(split, (0, 1, 3, 2, 4)).reshape(heads, 128, 128)]
  transfers between devices with their start and end apart: 78 -> 2, of which waited for: 38 -> 2; matrix products, arithmetic and copies ran while one was open for 30% -> 2% of each run, Pallas kernels for 0% -> 0%
where the time goes in v1:
time: 384 us; the launch traced here: 380 us
  Pallas kernels  219 us (57%)
  waiting for transfers between devices  80.5 us (21%)
  local copies, waits for them, and re-layouts  45.1 us (12%)
  other arithmetic  14.7 us (4%)
  between operations  13.6 us (4%)
  matrix products  7.73 us (2%)
    pallas_call x1, Pallas kernels, run_roles(): pl.pallas_call(role_kernel, out_shape=jax.ShapeDtypeStruct((N_TM, 128, 12...  115 us
    pallas_call x2, Pallas kernels, exchange(): pl.pallas_call(kernel, out_shape=jax.ShapeDtypeStruct(shape, B), in_specs...  104 us
    unnamed x3, waiting for transfers between devices  44.7 us
    all_gather x1, waiting for transfers between devices, local(): lax.all_gather(tokens, 'head', axis=1, tiled=True)  35.8 us
    unnamed x20, local copies, waits for them, and re-layouts  10.8 us
    convert_element_type x2, local copies, waits for them, and re-layouts, local(): unpair(exchange(gather_kernel, done, (3 * HEADS, 128, 128), 'collect', 2))  8.87 us
  transfers between devices with their start and end apart: 2, of which 2 were waited for; matrix products, arithmetic and copies ran while one was open for 2% of the time, Pallas kernels for 0%

profile of v1, /device:TPU:6, one launch (start us, length us, event | category | flops | bytes accessed | tf_op | source)
XLA Modules:
  0.0 380.3 jit_solution(7512486701647718478)
XLA Ops:
  7.3 1.3 tanh.3
  8.7 1.2 dynamic_slice.26.rate_ref
  10.6 1.5 convert_reduce_fusion.1
  12.1 1.4 pad_add_fusion.cut_ref
  16.7 35.8 %all-gather.2.cloned.1.call-done = bf16[256,3072]{1,0:T(8,128)(2,1)} async-done(((bf16[256,384]{1,0:T(8,128)(2,1)}), bf16[256,3072]{1,0:T(8,128)(2,1)}) %all-gather.2.cloned.1.call-update) | async-done | bytes 1572880 | tf_op jit(solution)/shard_map/all_gather | solution.py:364
  52.5 5.6 %fusion.2 = bf16[3,384,256]{2,1,0:T(8,128)(2,1)S(1)} fusion(bf16[3,3072,384]{2,1,0:T(8,128)(2,1)} %param.13, bf16[256,3072]{1,0:T(8,128)(2,1)} %all-gather.2.cloned.1.call-done), kind=kOutput, calls=%fused_computation.3 | convolution fusion | flops 1812234240 | bytes 9240576 | tf_op jit(solution)/shard_map/tw,cwf->ctf/dot_general | solution.py:362
  58.0 1.4 copy.39
  59.4 1.9 fusion.10
  61.4 2.3 slice_convert_fusion
  66.6 1.2 reshape.71
  67.8 2.2 copy.53
  70.0 1.9 reshape.72
  71.9 1.6 fusion.6
  73.6 2.4 maximum_maximum_fusion.src
  76.0 72.4 %spread.1.buf = bf16[32,384,128]{2,1,0:T(8,128)(2,1)} custom-call(bf16[12,384,128]{2,1,0:T(8,128)(2,1)} %maximum_maximum_fusion.src), custom_call_target="tpu_custom_call" | custom-call | tf_op jit(solution)/shard_map/spread/pallas_call | solution.py:299
  148.4 1.9 copy-done.1
  150.3 114.7 %roles.1.src = bf16[32,128,128]{2,1,0:T(8,128)(2,1)S(1)} custom-call(s32[2]{0:T(128)S(1)} %pad_add_fusion.cut_ref, f32[1]{0:T(128)} %dynamic_slice.26.rate_ref, bf16[32,384,128]{2,1,0:T(8,128)(2,1)S(1)} %copy-done.1, f32[128,256]{1,0:T(8,128)S(1)} %maximum_maximum_fusion.1.w1, f32[64,256]{1,0:T(8,128)S(1)} %dynamic-slice_bitcast_fusion.w2, ...), custom_call_target="tpu_custom_call" | custom-call | tf_op jit(solution)/shard_map/roles/pallas_call | solution.py:329
  266.0 31.6 %collect.1 = bf16[18,128,128]{2,1,0:T(8,128)(2,1)} custom-call(bf16[32,128,128]{2,1,0:T(8,128)(2,1)} %copy-done.2), custom_call_target="tpu_custom_call" | custom-call | tf_op jit(solution)/shard_map/collect/pallas_call | solution.py:299
  297.6 3.6 reshape.77
  301.2 5.3 %copy.42 = f32[18,2,64,2,64]{2,3,1,4,0:T(2,128)} copy(f32[18,2,64,2,64]{4,3,2,1,0:T(2,128)} %reshape.77) | data formatting | bytes 2359296 | tf_op jit(solution)/shard_map/convert_element_type | solution.py:408
  306.5 3.1 slice.37
  309.6 1.4 slice.36
  311.0 3.3 reshape.73
  314.3 1.9 fusion.18
  316.3 2.2 copy.50
  318.4 1.2 copy.51
  319.6 1.2 copy.43
  320.8 2.0 fusion.14
  323.0 2.2 convolution_convert_fusion
  325.1 2.6 copy.48
  327.7 44.0 %reduce-scatter.4.cloned.1.call-done = bf16[384,256]{1,0:T(8,128)(2,1)} async-done(((bf16[3072,256]{1,0:T(8,128)(2,1)}), bf16[384,256]{1,0:T(8,128)(2,1)}) %reduce-scatter.4.cloned.1.call-update) | async-done | bytes 196624
  371.7 1.7 copy.49
  (33 shorter events, 8.8 us)
Async XLA Ops:
  6.5 316.4 %copy-start = (bf16[384,3072]{1,0:T(8,128)(2,1)S(1)}, bf16[384,3072]{1,0:T(8,128)(2,1)}, u32[]{:S(2)}) copy-start(bf16[384,3072]{1,0:T(8,128)(2,1)} %param.14) | copy-start | bytes 7077892
  6.5 45.9 %all-gather.2.cloned.1.call-start = ((), (), s32[]{:S(2)}) async-start(), calls=%async_computation.1 | async-start | bytes 1769472 | tf_op jit(solution)/shard_map/all_gather | solution.py:364
  7.3 364.5 %reduce-scatter.4.cloned.1.call-start = ((), (), s32[]{:S(2)}) async-start(), calls=%async_computation.2 | async-start | bytes 1769472
  64.8 0.6 copy-start.5
  65.4 8.1 %copy-start.3 = (bf16[6,256,64]{2,1,0:T(8,128)(2,1)S(1)}, bf16[6,256,64]{2,1,0:T(8,128)(2,1)}, u32[]{:S(2)}) copy-start(bf16[6,256,64]{2,1,0:T(8,128)(2,1)} %get-tuple-element.14) | copy-start | bytes 589828
  65.4 8.1 %copy-start.4 = (bf16[6,256,64]{2,1,0:T(8,128)(2,1)S(1)}, bf16[6,256,64]{2,1,0:T(8,128)(2,1)}, u32[]{:S(2)}) copy-start(bf16[6,256,64]{2,1,0:T(8,128)(2,1)} %get-tuple-element.15) | copy-start | bytes 589828
  148.4 1.9 copy-start.1
  265.0 1.0 copy-start.2
  316.3 4.5 %copy-start.6 = (f32[6,256]{1,0:T(8,128)S(1)}, f32[6,256]{1,0:T(8,128)}, u32[]{:S(2)}) copy-start(f32[6,256]{1,0:T(8,128)} %copy-done.5) | copy-start | bytes 18436
  316.3 4.5 %copy-start.7 = (f32[6,64]{1,0:T(8,128)S(1)}, f32[6,64]{1,0:T(8,128)}, u32[]{:S(2)}) copy-start(f32[6,64]{1,0:T(8,128)} %tanh.3) | copy-start | bytes 4612
Sparse Core Ops, SparseCore 0:
  9.2 43.2 all-gather.1
  327.9 43.8 reduce-scatter.3

commit v2 on v1

v2 whole, which is shorter than its diff:
```python
import jax
import jax.numpy as jnp
from jax import lax
from jax.experimental import pallas as pl
from jax.experimental.pallas import tpu as pltpu
from jax.sharding import PartitionSpec as P

MESH = pl.DeviceIdType.MESH
F = jnp.float32
B = jnp.bfloat16
HDIM = 64
GROUP = 64
EPS = 1e-06
NN = (((1,), (0,)), ((), ()))
NT = (((1,), (1,)), ((), ()))
TN = (((0,), (0,)), ((), ()))
C0 = 0.7978845608028654
C1 = 0.044715
N_TM = 32
HEADS = 6
BLOCKS = 128
PACK = 384
KEYS = 2048
CHAINS = 2 * HEADS
PER_HEAD = 3
ROLES = CHAINS + PER_HEAD * HEADS
N_HEAD = 8
WIDTH = HEADS * HDIM


def mm(a, b, dims=NN):
    return lax.dot_general(a, b, dims, preferred_element_type=F)


def gelu_both(x):
    x2 = x * x
    th = jnp.tanh(x * (C0 + (C0 * C1) * x2))
    hp = 0.5 + 0.5 * th
    return x * hp, hp + (hp - hp * hp) * (x * (2 * C0 + (6 * C0 * C1) * x2))


def gelu(x):
    x2 = x * x
    th = jnp.tanh(x * (C0 + (C0 * C1) * x2))
    return x * (0.5 + 0.5 * th)


def mean(x):
    return jnp.mean(x, -1, keepdims=True)


def lanes(shape):
    return lax.broadcasted_iota(jnp.int32, shape, 1)


def chain(rev, rate, buf, w1, b1, w2, b2i, gn, bs, out, W1, W2, W2b, b2, arrived, finished):
    g2 = gn * gn
    s = rate / (GROUP * HDIM)
    lane = lanes((64, 128))
    tail = jnp.where(lane == 64, 1.0, 0.0).astype(B)

    def place(step):
        b = jnp.clip(step, 0, BLOCKS - 1)
        b = jnp.where(rev, BLOCKS - 1 - b, b)
        return b // 4, b % 4

    def load_ka(step):
        i, j = place(step)
        return buf[i, pl.ds(pl.multiple_of(j * 64, 64), 64), :]

    def load_q(step):
        i, j = place(step)
        both = buf[i, pl.ds(pl.multiple_of(256 + (j // 2) * 64, 64), 64), :]
        swapped = jnp.concatenate([both[:, 64:], both[:, :64]], 1)
        return jnp.where(lane < 64, jnp.where(j % 2 == 0, both, swapped), tail)

    def augment(ka):
        return jnp.where(lane < 64, ka, tail)

    arrived(0)
    W1[0:64] = w1
    W1[64:128] = jnp.where(lax.broadcasted_iota(jnp.int32, (64, 256), 0) == 0, b1, 0.0)
    w2 = w2.T
    W2[...] = w2 - jnp.mean(w2, 0, keepdims=True)
    W2b[...] = W2[...].astype(B)
    valid = lane < 64
    valid_row = lanes((1, 128)) < 64

    def widen(x):
        return jnp.concatenate([x, jnp.zeros_like(x)], 1)

    def swap(x):
        return jnp.concatenate([x[:, 64:], x[:, :64]], 1)

    def rowsum(x):
        return jnp.sum(x, -1, keepdims=True) * (1.0 / HDIM)

    b2[...] = widen(b2i - mean(b2i))
    gn, bs, g2 = widen(gn), widen(bs), widen(g2)
    first = augment(load_ka(0))
    base0 = mm(first, W1[...].astype(B))
    zero_rows = jnp.zeros((64, 256), B)

    def body(t, carry):
        G1, base, Pt, KTs, Kt, Zlast = carry
        Ab = jnp.where(valid, swap(load_ka(t)), jnp.zeros((64, 128), B))
        A = Ab.astype(F)
        W2t = W2b[...]
        W2z = jnp.concatenate([W2t, zero_rows], 0)
        b2t = b2[...]
        AW = mm(Ab[:, :64], W2t)
        R = mm(jnp.concatenate([Pt, KTs], 0), G1)
        Z1 = base - R[:64]
        W1n = W1[...] - R[64:]
        W1[...] = W1n
        W1b = W1n.astype(B)
        X2, dX = gelu_both(Z1)
        X2b = X2.astype(B)
        Z = mm(X2b, W2z, NT) + b2t
        Zg = Z * g2
        D = mm(jnp.concatenate([Zg.astype(B), Z.astype(B)], 0)[:, :64], W2t)
        mA = rowsum(A)
        S1, S2, S3, S4 = rowsum(Z * Z), rowsum(Zg), rowsum(Z * Zg), rowsum(A * Z)
        inv = lax.rsqrt(S1 + EPS)
        a1 = inv * inv
        a3 = a1 * (a1 * S3 + inv * S4)
        G1n = ((a1 * D[:64] + inv * AW - a3 * D[64:]) * dX).astype(B)
        G2 = a1 * Zg + inv * A - a3 * Z - inv * (inv * S2 + mA)
        U = mm(G2.astype(B)[:, :64], X2b, TN)
        W2n = W2[...] - s * U
        W2b[...] = W2n.astype(B)
        W2[...] = W2n - jnp.mean(W2n, 0, keepdims=True)
        b2n = jnp.where(valid_row, b2t - s * jnp.sum(G2, 0, keepdims=True), 0.0)
        b2[...] = jnp.where(valid_row, b2n - rowsum(b2n), 0.0)
        Kn = augment(load_ka(t + 1))
        Y = mm(jnp.concatenate([load_q(t - 1), Kn], 0), W1b)
        Zq = mm(gelu(Y[:64]).astype(B), W2z, NT) + b2t
        Pn = (s * mm(Kn, Kt, NT)).astype(B)
        KTn = (s * Kt.astype(F)).T.astype(B)
        z = jnp.where(valid, Zlast - rowsum(Zlast), 0.0)
        o = (z * lax.rsqrt(rowsum(z * z) + EPS) * gn + bs).astype(B)
        i, j = place(t - 2)
        rows = pl.ds(pl.multiple_of((j // 2) * 64, 64), 64)
        out[i, rows, :] = jnp.where(valid == (j % 2 == 0), jnp.where(j % 2 == 0, o, swap(o)), out[i, rows, :])
        return G1n, Y[64:], Pn, KTn, Kn, Zq

    def group(i, carry):
        @pl.when(i + 1 < N_TM)
        def _():
            arrived(i + 1)

        carry = lax.fori_loop(4 * i, 4 * i + 4, body, carry)

        @pl.when(i > 0)
        def _():
            finished(i - 1)

        return carry

    carry = lax.fori_loop(
        0,
        N_TM,
        group,
        (
            jnp.zeros((64, 256), B),
            base0,
            jnp.zeros((64, 64), B),
            jnp.zeros((128, 64), B),
            first,
            jnp.zeros((64, 128), F),
        ),
    )
    lax.fori_loop(BLOCKS, BLOCKS + 2, body, carry)
    finished(N_TM - 1)


def third_begin(third):
    return (third * N_TM + PER_HEAD - 1) // PER_HEAD


def attend(third, ids, buf, out, finished):
    begin, end = third_begin(third), third_begin(third + 1)
    lane = lanes((128, 128))
    low = lane < 64
    per = KEYS // 256

    def count(flags):
        ones_of = jnp.where(flags, 1.0, 0.0)
        return jnp.sum(jnp.sum(ones_of, 0, keepdims=True), 1, keepdims=True)

    c1, c2 = count(ids < 1), count(ids < 2)

    def segment(pos):
        pos = pos.astype(F)
        return jnp.where(pos >= c1, 1.0, 0.0) + jnp.where(pos >= c2, 1.0, 0.0)

    row = lax.broadcasted_iota(jnp.int32, (256, 1), 0)
    inside = (row % 128) // 64 * 128 + (row // 128) * 64 + row % 64

    def block(i, _):
        both = buf[i, 256:PACK, :]
        swapped = jnp.concatenate([both[:, 64:], both[:, :64]], 1)
        zero = jnp.zeros_like(both)
        q = jnp.concatenate([jnp.where(low, both, zero), jnp.where(low, swapped, zero)], 0)
        own = segment(i * 256 + inside)

        def keys(n, carry):
            top, acc, total = carry
            kv = jnp.concatenate([buf[n * per + m, 0:256, :] for m in range(per)], 0)
            scores = mm(q, kv, NT)
            ids = segment(n * KEYS + lanes((1, KEYS)))
            scores = jnp.where(own == ids, scores, -1e30)
            top_new = jnp.maximum(top, jnp.max(scores, -1, keepdims=True))
            w = jnp.exp(scores - top_new)
            fade = jnp.exp(top - top_new)
            total = total * fade + jnp.sum(w, -1, keepdims=True)
            return top_new, acc * fade + mm(w.astype(B), kv), total

        start = (jnp.full((256, 1), -1e30, F), jnp.zeros((256, 128), F), jnp.zeros((256, 1), F))
        _, acc, total = lax.fori_loop(0, N_TM * 256 // KEYS, keys, start)
        o = acc / total
        lo = jnp.concatenate([o[:128, 64:], o[:128, :64]], 1)
        out[i] = jnp.where(low, lo, o[128:]).astype(B)
        finished(i)
        return 0

    lax.fori_loop(begin, end, block, 0)


def greet(axis):
    me, n = lax.axis_index(axis), lax.axis_size(axis)
    barrier = pltpu.get_barrier_semaphore()

    @pl.loop(1, n)
    def _(k):
        pl.semaphore_signal(
            barrier, inc=1, device_id={axis: lax.rem(me + k, n)}, device_id_type=MESH
        )

    pl.semaphore_wait(barrier, n - 1)
    return me


def slot_of(d):
    return jnp.where(d < CHAINS, d // 2, HEADS + (d - CHAINS) // PER_HEAD)


def with_queries(block, d):
    third = (d - CHAINS) % PER_HEAD
    return (d < CHAINS) | ((block >= third_begin(third)) & (block < third_begin(third + 1)))


def sweep_kernel(
    src, rate, ids, w1, b1, w2, b2i, gain, bias, res,
    buf, out, W1, W2, W2b, b2, send_sem, recv_sem, own_sem, res_send, res_recv,
):
    me = greet("tm")
    short = pl.ds(0, 256)

    def parcel(d, part):
        slot = slot_of(d)
        return pltpu.make_async_remote_copy(
            src_ref=src.at[slot, short] if part else src.at[slot],
            dst_ref=buf.at[me, short] if part else buf.at[me],
            send_sem=send_sem.at[d],
            recv_sem=recv_sem.at[me],
            device_id={"tm": d},
            device_id_type=MESH,
        )

    def each(first, count, stride, act):
        @pl.loop(0, count)
        def _(k):
            d = first + stride * k

            @pl.when(d != me)
            def _():
                act(d)

    def start(d):
        @pl.when(with_queries(me, d))
        def _():
            parcel(d, False).start()

        @pl.when(jnp.logical_not(with_queries(me, d)))
        def _():
            parcel(d, True).start()

    def sent(d):
        @pl.when(with_queries(me, d))
        def _():
            parcel(d, False).wait_send()

        @pl.when(jnp.logical_not(with_queries(me, d)))
        def _():
            parcel(d, True).wait_send()

    @pl.when(me < ROLES)
    def _():
        own = pltpu.make_async_copy(src.at[slot_of(me)], buf.at[me], own_sem)
        own.start()
        own.wait()

    early, late = me < 8, me >= 24
    each(jnp.where(late, 1, 0), jnp.where(early | late, HEADS, 0), 2, start)
    each(CHAINS, PER_HEAD * HEADS, 1, start)
    each(jnp.where(me < 16, 0, 1), jnp.where(early | late, 0, HEADS), 2, start)
    each(jnp.where(me < 16, 1, 0), HEADS, 2, start)

    def landed(i):
        @pl.when(i != me)
        def _():
            @pl.when(with_queries(i, me))
            def _():
                pltpu.make_async_copy(buf.at[i], buf.at[i], recv_sem.at[i]).wait()

            @pl.when(jnp.logical_not(with_queries(i, me)))
            def _():
                got = buf.at[i, short]
                pltpu.make_async_copy(got, got, recv_sem.at[i]).wait()

    slot = jnp.where(me < CHAINS, me, CHAINS + (me - CHAINS) // PER_HEAD)

    def away(i):
        return pltpu.make_async_remote_copy(
            src_ref=out.at[i],
            dst_ref=res.at[slot],
            send_sem=res_send.at[i],
            recv_sem=res_recv.at[slot],
            device_id={"tm": i},
            device_id_type=MESH,
        )

    def here(i):
        return pltpu.make_async_copy(out.at[i], res.at[slot], res_send.at[i])

    def deliver(i):
        @pl.when(i != me)
        def _():
            away(i).start()

        @pl.when(i == me)
        def _():
            here(i).start()

    def delivered(i):
        @pl.when(i != me)
        def _():
            away(i).wait_send()

        @pl.when(i == me)
        def _():
            here(i).wait()

    @pl.when(me < CHAINS)
    def _():
        rev = me % 2 == 1
        head = me // 2
        row = pl.ds(head, 1)

        def real(i):
            return jnp.where(rev, N_TM - 1 - i, i)

        chain(
            rev, rate[head], buf, w1[head], b1[row, :], w2[head], b2i[row, :], gain[row, :], bias[row, :],
            out, W1, W2, W2b, b2, lambda i: landed(real(i)), lambda i: deliver(real(i)),
        )
        pl.loop(0, N_TM)(delivered)

    @pl.when((me >= CHAINS) & (me < ROLES))
    def _():
        third = (me - CHAINS) % PER_HEAD
        pl.loop(0, N_TM)(landed)
        attend(third, ids[...], buf, out, deliver)
        pl.loop(third_begin(third), third_begin(third + 1))(delivered)

    each(0, ROLES, 1, sent)

    @pl.loop(0, 3 * HEADS)
    def _(slot):
        third = jnp.where(me < third_begin(1), 0, jnp.where(me < third_begin(2), 1, 2))
        origin = jnp.where(slot < CHAINS, slot, CHAINS + (slot - CHAINS) * PER_HEAD + third)

        @pl.when(origin != me)
        def _():
            pltpu.make_async_copy(res.at[slot], res.at[slot], res_recv.at[slot]).wait()


def tile_row(ref, g):
    return jnp.concatenate([ref[2 * g : 2 * g + 1, :], ref[2 * g + 1 : 2 * g + 2, :]], 1)


def swap_halves(x):
    return jnp.concatenate([x[:, 64:], x[:, :64]], 1)


def project_kernel(tok, w_hbm, gain, bias, src, qrows, toks, w, acc, send_sem, recv_sem, w_sem):
    me = lax.axis_index("head")
    fetch = pltpu.make_async_copy(w_hbm, w, w_sem)
    fetch.start()
    greet("head")

    def parcel(k):
        return pltpu.make_async_remote_copy(
            src_ref=tok,
            dst_ref=toks.at[me],
            send_sem=send_sem.at[k],
            recv_sem=recv_sem.at[me],
            device_id={"head": lax.rem(me + k, N_HEAD)},
            device_id_type=MESH,
        )

    pl.loop(1, N_HEAD)(lambda k: parcel(k).start())
    fetch.wait()

    def add(x, s, fresh):
        rows = pl.ds(pl.multiple_of(s * WIDTH, WIDTH), WIDTH)
        for c in range(3):
            cols = slice(c * WIDTH, (c + 1) * WIDTH)
            y = mm(x, w[c, rows, :])
            acc[:, cols] = y if fresh else acc[:, cols] + y

    add(tok[...], me, True)

    @pl.loop(1, N_HEAD)
    def _(k):
        s = lax.rem(me + N_HEAD - k, N_HEAD)
        pltpu.make_async_copy(toks.at[s], toks.at[s], recv_sem.at[s]).wait()
        add(toks[s], s, False)

    low = lanes((256, 128)) < 64
    low_half = lanes((128, 128)) < 64
    r = lax.broadcasted_iota(jnp.int32, (128, 128), 0)
    same = jnp.where((r < 64) == low_half, 1.0 / HDIM, 0.0).astype(B)

    def scaled(x):
        sq = x * x
        hi = sq.astype(B)
        return x * lax.rsqrt(mm(hi, same) + mm((sq - hi.astype(F)).astype(B), same) + EPS)

    def pack_rows(left, right):
        pairs = [jnp.where(low, left, swap_halves(right)), jnp.where(low, swap_halves(left), right)]
        return pairs

    def pack_pairs(x):
        y = swap_halves(x)
        even = [jnp.where(low[:64], x[a : a + 64], y[a + 64 : a + 128]) for a in (0, 128)]
        odd = [jnp.where(low[:64], y[a : a + 64], x[a + 64 : a + 128]) for a in (0, 128)]
        return jnp.concatenate(even, 0), jnp.concatenate(odd, 0)

    for g in range(HEADS // 2):
        q, k, v = (
            acc[:, c * WIDTH + g * 128 : c * WIDTH + (g + 1) * 128].astype(B).astype(F) for c in range(3)
        )
        qn, kn, vn = scaled(q), scaled(k), scaled(v)
        qrows[:, g * 128 : (g + 1) * 128] = qn
        aim = (tile_row(bias, g) - (vn - kn)) * tile_row(gain, g)
        sets = ((kn, aim, qn, 0), (k, v, q * HDIM**-0.5, HEADS))
        for left, right, quer, offset in sets:
            tops, tails = pack_rows(left, right), pack_pairs(quer)
            for e in range(2):
                src[offset + 2 * g + e, 0:256, :] = tops[e].astype(B)
                src[offset + 2 * g + e, 256:PACK, :] = tails[e].astype(B)

    pl.loop(1, N_HEAD)(lambda k: parcel(k).wait_send())


def finish_kernel(res, qrows, gate, w, out, mixed, terms, got, send_sem, recv_sem):
    me = greet("head")
    low = lanes((64, 128)) < 64
    for g in range(HEADS // 2):
        weight = jnp.tanh(tile_row(gate, g))
        for p in range(2):
            rows = slice(p * 64, p * 64 + 64)
            both = []
            for e in range(2):
                h = 2 * g + e
                swept = res[2 * h, rows, :].astype(F) + res[2 * h + 1, rows, :].astype(F)
                both.append((swept, res[CHAINS + h, rows, :].astype(F)))
            for c in range(2):
                at = slice((2 * p + c) * 64, (2 * p + c + 1) * 64)
                swept, attention = (
                    jnp.where(low, x, swap_halves(y)) if c == 0 else jnp.where(low, swap_halves(x), y)
                    for x, y in zip(both[0], both[1])
                )
                cols = slice(g * 128, g * 128 + 128)
                mixed[at, cols] = (attention + weight * (swept + 2.0 * qrows[at, cols])).astype(B)

    def part(d):
        cols = pl.ds(pl.multiple_of(d * WIDTH, WIDTH), WIDTH)
        return mm(mixed[...], w[:, cols])

    def parcel(k):
        return pltpu.make_async_remote_copy(
            src_ref=terms.at[k],
            dst_ref=got.at[me],
            send_sem=send_sem.at[k],
            recv_sem=recv_sem.at[me],
            device_id={"head": lax.rem(me + k, N_HEAD)},
            device_id_type=MESH,
        )

    @pl.loop(1, N_HEAD)
    def _(k):
        terms[k] = part(lax.rem(me + k, N_HEAD)).astype(B)
        parcel(k).start()

    def gather(k, total):
        s = lax.rem(me + N_HEAD - k, N_HEAD)
        pltpu.make_async_copy(got.at[s], got.at[s], recv_sem.at[s]).wait()
        return total + got[s].astype(F)

    out[...] = lax.fori_loop(1, N_HEAD, gather, part(me)).astype(B)
    pl.loop(1, N_HEAD)(lambda k: parcel(k).wait_send())


def call(kernel, shapes, memory, scratch, name, collective_id):
    several = len(shapes) > 1
    spaces = {"v": pltpu.VMEM, "s": pltpu.SMEM, "h": pl.ANY}
    ins, outs = memory
    specs = [pl.BlockSpec(memory_space=spaces[m]) for m in outs]
    return pl.pallas_call(
        kernel,
        out_shape=shapes if several else shapes[0],
        in_specs=[pl.BlockSpec(memory_space=spaces[m]) for m in ins],
        out_specs=specs if several else specs[0],
        scratch_shapes=scratch,
        compiler_params=pltpu.CompilerParams(
            collective_id=collective_id, has_side_effects=True, vmem_limit_bytes=48 * 2**20
        ),
        name=name,
    )


def local(
    tokens,
    qkv_weight,
    out_weight,
    segment_ids,
    inner_w1,
    inner_b1,
    inner_w2,
    inner_b2,
    norm_gain,
    norm_bias,
    inner_rate,
    out_gate,
):
    rows = tokens.shape[0]
    dma = pltpu.SemaphoreType.DMA
    src, qrows = call(
        project_kernel,
        [
            jax.ShapeDtypeStruct((2 * HEADS, PACK, 128), B),
            jax.ShapeDtypeStruct((rows, WIDTH), F),
        ],
        ("vhvv", "vv"),
        [
            pltpu.VMEM((N_HEAD, rows, WIDTH), B),
            pltpu.VMEM(qkv_weight.shape, B),
            pltpu.VMEM((rows, 3 * WIDTH), F),
            dma((N_HEAD,)),
            dma((N_HEAD,)),
            dma,
        ],
        "project",
        1,
    )(tokens, qkv_weight, norm_gain, norm_bias)
    res = call(
        sweep_kernel,
        [jax.ShapeDtypeStruct((3 * HEADS, 128, 128), B)],
        ("vs" + "v" * 7, "h"),
        [
            pltpu.VMEM((N_TM, PACK, 128), B),
            pltpu.VMEM((N_TM, 128, 128), B),
            pltpu.VMEM((128, 256), F),
            pltpu.VMEM((64, 256), F),
            pltpu.VMEM((64, 256), B),
            pltpu.VMEM((1, 128), F),
            dma((N_TM,)),
            dma((N_TM,)),
            dma,
            dma((N_TM,)),
            dma((3 * HEADS,)),
        ],
        "sweep",
        2,
    )(
        src,
        inner_rate,
        segment_ids.reshape(64, 128),
        inner_w1,
        inner_b1,
        inner_w2,
        inner_b2,
        norm_gain,
        norm_bias,
    )
    return call(
        finish_kernel,
        [jax.ShapeDtypeStruct((rows, WIDTH), B)],
        ("vvvv", "v"),
        [
            pltpu.VMEM((rows, WIDTH), B),
            pltpu.VMEM((N_HEAD, rows, WIDTH), B),
            pltpu.VMEM((N_HEAD, rows, WIDTH), B),
            dma((N_HEAD,)),
            dma((N_HEAD,)),
        ],
        "finish",
        3,
    )(res, qrows, out_gate, out_weight)


def solution(mesh):
    placed = (
        P("tm", "head"),
        P(None, None, "head"),
        P("head", None),
        P(),
        P("head", None, None),
        P("head", None),
        P("head", None, None),
        P("head", None),
        P("head", None),
        P("head", None),
        P("head"),
        P("head", None),
    )
    return jax.shard_map(
        local, mesh=mesh, in_specs=placed, out_specs=P("tm", "head"), check_vma=False
    )
```

time: 384 us -> 186 us (0.48)
  waiting for transfers between devices: 80.5 us -> 0 us
  local copies, waits for them, and re-layouts: 45.1 us -> 4.27 us
  Pallas kernels: 219 us -> 180 us
  other arithmetic: 14.7 us -> 0 us
  between operations: 13.6 us -> 0.13 us
  matrix products: 7.73 us -> 0 us
    unnamed x3 -> x0, waiting for transfers between devices: 44.7 us -> none
    pallas_call x3, Pallas kernels: 219 us -> 180 us  [the longest x1 126 us: local(): call(sweep_kernel, [jax.ShapeDtypeStruct((3 * HEADS, 128, 128), B)], ('vs...]
    all_gather x1 -> x0, waiting for transfers between devices: 35.8 us -> none  [local(): lax.all_gather(tokens, 'head', axis=1, tiled=True)]
    convert_element_type x2 -> x0, local copies, waits for them, and re-layouts: 8.87 us -> none  [local(): unpair(exchange(gather_kernel, done, (3 * HEADS, 128, 128), 'collect', 2))]
    reshape x4 -> x0, local copies, waits for them, and re-layouts: 7.83 us -> none  [the longest x1 3.31 us: local(): sweeps = res[:CHAINS].reshape(heads, 2, rows, HDIM)]
    dot_general x2 -> x0, matrix products: 7.73 us -> none  [the longest x1 5.57 us: local(): jnp.einsum('tw,cwf->ctf', lax.all_gather(tokens, 'head', axis=1, tiled=Tr...]
    slice x4 -> x0, local copies, waits for them, and re-layouts: 7.65 us -> none  [the longest x1 3.14 us: local(): sweeps = res[:CHAINS].reshape(heads, 2, rows, HDIM)]
    unnamed x20 -> x22, local copies, waits for them, and re-layouts: 10.8 us -> 4.27 us
  transfers between devices with their start and end apart: 2 -> 0, of which waited for: 2 -> 0; matrix products, arithmetic and copies ran while one was open for 2% -> 0% of each run, Pallas kernels for 0% -> 0%
where the time goes in v2:
time: 186 us; the launch traced here: 185 us
  Pallas kernels  180 us (97%)
  local copies, waits for them, and re-layouts  4.27 us (2%)
    pallas_call x1, Pallas kernels, local(): call(sweep_kernel, [jax.ShapeDtypeStruct((3 * HEADS, 128, 128), B)], ('vs...  126 us
    pallas_call x1, Pallas kernels, local(): call(project_kernel, [jax.ShapeDtypeStruct((2 * HEADS, PACK, 128), B), ja...  28.1 us
    pallas_call x1, Pallas kernels, local(): call(finish_kernel, [jax.ShapeDtypeStruct((rows, WIDTH), B)], ('vvvv', 'v...  26.1 us
    unnamed x22, local copies, waits for them, and re-layouts  4.27 us

profile of v2, /device:TPU:6, one launch (start us, length us, event | category | flops | bytes accessed | tf_op | source)
XLA Modules:
  0.0 184.5 jit_solution(18211967444146104336)
XLA Ops:
  0.0 1.3 copy.13.w2
  1.3 0.0 copy-start.2
  1.3 0.9 copy-done.2
  2.2 0.0 copy-start.4
  2.2 0.7 copy-done.4
  2.9 0.0 copy-start.5
  2.9 0.7 copy-done.5
  3.6 0.0 copy-start.1
  3.6 0.0 copy-start.3
  3.6 0.0 copy-start.6
  3.6 0.0 copy-start.7
  3.6 0.0 copy-start.9
  3.6 28.1 %project.1 = (bf16[12,384,128]{2,1,0:T(8,128)(2,1)S(1)}, f32[256,384]{1,0:T(8,128)S(1)}) custom-call(bf16[256,384]{1,0:T(8,128)(2,1)S(1)} %copy-done.2, bf16[3,3072,384]{2,1,0:T(8,128)(2,1)} %w_hbm.1, f32[6,64]{1,0:T(8,128)S(1)} %copy-done.4, f32[6,64]{1,0:T(8,128)S(1)} %copy-done.5), custom_call_target="tpu_custom_call" | custom-call | tf_op jit(solution)/shard_map/project/pallas_call | solution.py:551
  31.7 0.0 copy-start
  31.7 0.0 copy-start.8
  31.7 0.0 copy-done.1
  31.7 0.0 copy-done.3
  31.7 0.0 copy-done.6
  31.7 0.0 copy-done.7
  31.7 0.0 copy-done.9
  31.7 125.9 %sweep.1.res = bf16[18,128,128]{2,1,0:T(8,128)(2,1)S(1)} custom-call(bf16[12,384,128]{2,1,0:T(8,128)(2,1)S(1)} %get-tuple-element.7.src, f32[6]{0:T(128)S(1)} %copy-done.9, s32[64,128]{1,0:T(8,128)S(1)} %bitcast.1, f32[6,64,256]{2,1,0:T(8,128)S(1)} %copy-done.1, f32[6,256]{1,0:T(8,128)S(1)} %copy-done.6, f32[6,256,64]{2,1,0:T(8,128)S(1)} %copy.13.w2, ...), custom_call_target="tpu_custom_call" | custom-call | tf_op jit(solution)/shard_map/sweep/pallas_call | solution.py:569
  157.7 0.0 copy-done
  157.7 0.0 copy-done.8
  157.7 26.1 %finish.1 = bf16[256,384]{1,0:T(8,128)(2,1)S(1)} custom-call(bf16[18,128,128]{2,1,0:T(8,128)(2,1)S(1)} %sweep.1.res, f32[256,384]{1,0:T(8,128)S(1)} %get-tuple-element.8.qrows, f32[6,64]{1,0:T(8,128)S(1)} %copy-done.8, bf16[384,3072]{1,0:T(8,128)(2,1)S(1)} %copy-done), custom_call_target="tpu_custom_call" | custom-call | tf_op jit(solution)/shard_map/finish/pallas_call | solution.py:599
  183.8 0.7 copy.15
Async XLA Ops:
  1.3 0.9 copy-start.2
  2.2 0.7 copy-start.4
  2.9 0.7 copy-start.5
  3.6 28.1 %copy-start.1 = (f32[6,64,256]{2,1,0:T(8,128)S(1)}, f32[6,64,256]{2,1,0:T(8,128)}, u32[]{:S(2)}) copy-start(f32[6,64,256]{2,1,0:T(8,128)} %w1.1) | copy-start | bytes 1179652
  3.6 28.1 %copy-start.3 = (s32[8192]{0:T(1024)S(1)}, s32[8192]{0:T(1024)}, u32[]{:S(2)}) copy-start(s32[8192]{0:T(1024)} %param.15) | copy-start | bytes 98308
  3.6 28.1 %copy-start.6 = (f32[6,256]{1,0:T(8,128)S(1)}, f32[6,256]{1,0:T(8,128)}, u32[]{:S(2)}) copy-start(f32[6,256]{1,0:T(8,128)} %b1.1) | copy-start | bytes 18436
  3.6 28.1 %copy-start.7 = (f32[6,64]{1,0:T(8,128)S(1)}, f32[6,64]{1,0:T(8,128)}, u32[]{:S(2)}) copy-start(f32[6,64]{1,0:T(8,128)} %b2i.1) | copy-start | bytes 4612
  3.6 28.2 %copy-start.9 = (f32[6]{0:T(128)S(1)}, f32[6]{0:T(128)}, u32[]{:S(2)}) copy-start(f32[6]{0:T(128)} %rate.1) | copy-start | bytes 76
  31.7 126.0 %copy-start = (bf16[384,3072]{1,0:T(8,128)(2,1)S(1)}, bf16[384,3072]{1,0:T(8,128)(2,1)}, u32[]{:S(2)}) copy-start(bf16[384,3072]{1,0:T(8,128)(2,1)} %w.1) | copy-start | bytes 7077892
  31.7 126.0 %copy-start.8 = (f32[6,64]{1,0:T(8,128)S(1)}, f32[6,64]{1,0:T(8,128)}, u32[]{:S(2)}) copy-start(f32[6,64]{1,0:T(8,128)} %gate.1) | copy-start | bytes 4612

commit v3 on v2

--- a/solution.py
+++ b/solution.py
@@ -20,10 +20,12 @@
 HEADS = 6
 BLOCKS = 128
 PACK = 384
-KEYS = 2048
 CHAINS = 2 * HEADS
-PER_HEAD = 3
-ROLES = CHAINS + PER_HEAD * HEADS
+PLACES = 2 * HEADS
+HALF = N_TM // 2
+WINDOW = 4096 // 256 + 1
+UNITS = HALF + 2
+FAR = 1 << 20
 N_HEAD = 8
 WIDTH = HEADS * HDIM
 
@@ -174,57 +176,67 @@
     finished(N_TM - 1)
 
 
-def third_begin(third):
-    return (third * N_TM + PER_HEAD - 1) // PER_HEAD
-
-
-def attend(third, ids, buf, out, finished):
-    begin, end = third_begin(third), third_begin(third + 1)
-    lane = lanes((128, 128))
-    low = lane < 64
-    per = KEYS // 256
-
-    def count(flags):
-        ones_of = jnp.where(flags, 1.0, 0.0)
-        return jnp.sum(jnp.sum(ones_of, 0, keepdims=True), 1, keepdims=True)
-
-    c1, c2 = count(ids < 1), count(ids < 2)
-
-    def segment(pos):
-        pos = pos.astype(F)
-        return jnp.where(pos >= c1, 1.0, 0.0) + jnp.where(pos >= c2, 1.0, 0.0)
-
+def first_at_least(ids, value):
+    found = jnp.int32(0)
+    for bit in range(13, -1, -1):
+        trial = found + (1 << bit)
+        last = ids[jnp.minimum(trial, N_TM * 256) - 1]
+        found = jnp.where((trial <= N_TM * 256) & (last < value), trial, found)
+    return found
+
+
+def attend(half, ids, buf, parts, out, finished):
+    c1, c2 = first_at_least(ids, 1), first_at_least(ids, 2)
+    begin = half * HALF
+    low = lanes((128, 128)) < 64
     row = lax.broadcasted_iota(jnp.int32, (256, 1), 0)
     inside = (row % 128) // 64 * 128 + (row // 128) * 64 + row % 64
 
-    def block(i, _):
+    def segment(pos):
+        return jnp.where(pos >= c1, 1, 0) + jnp.where(pos >= c2, 1, 0)
+
+    def edge(number):
+        return jnp.where(number <= 0, 0, jnp.where(number == 1, c1, jnp.where(number == 2, c2, FAR)))
+
+    s0 = segment(begin * 256)
+    next1, next2 = edge(s0 + 1) // 256, edge(s0 + 2) // 256
+
+    def unit(u, _):
+        above = jnp.where(begin + u - 1 >= next1, 1, 0) + jnp.where(begin + u - 2 >= next2, 1, 0)
+        i = jnp.clip(begin + u - above, begin, begin + HALF - 1)
+        left, right = edge(s0 + above), edge(s0 + above + 1)
+        first = jnp.minimum(left // 256, N_TM - WINDOW)
         both = buf[i, 256:PACK, :]
         swapped = jnp.concatenate([both[:, 64:], both[:, :64]], 1)
         zero = jnp.zeros_like(both)
         q = jnp.concatenate([jnp.where(low, both, zero), jnp.where(low, swapped, zero)], 0)
-        own = segment(i * 256 + inside)
-
-        def keys(n, carry):
-            top, acc, total = carry
-            kv = jnp.concatenate([buf[n * per + m, 0:256, :] for m in range(per)], 0)
-            scores = mm(q, kv, NT)
-            ids = segment(n * KEYS + lanes((1, KEYS)))
-            scores = jnp.where(own == ids, scores, -1e30)
-            top_new = jnp.maximum(top, jnp.max(scores, -1, keepdims=True))
-            w = jnp.exp(scores - top_new)
-            fade = jnp.exp(top - top_new)
-            total = total * fade + jnp.sum(w, -1, keepdims=True)
-            return top_new, acc * fade + mm(w.astype(B), kv), total
-
-        start = (jnp.full((256, 1), -1e30, F), jnp.zeros((256, 128), F), jnp.zeros((256, 1), F))
-        _, acc, total = lax.fori_loop(0, N_TM * 256 // KEYS, keys, start)
-        o = acc / total
+        kv = buf[pl.ds(first, WINDOW), 0:256, :].reshape(WINDOW * 256, 128)
+        pos = first * 256 + lanes((1, WINDOW * 256))
+        scores = mm(q, kv, NT) + jnp.where((pos >= left) & (pos < right), 0.0, -1e30)
+        w = jnp.exp(scores - jnp.max(scores, -1, keepdims=True))
+        total = jnp.sum(w, -1, keepdims=True)
+        parts[u] = mm(w.astype(B), kv) / total
+        return 0
+
+    lax.fori_loop(0, UNITS, unit, 0)
+
+    def assemble(i, _):
+        s1 = segment(i * 256)
+        mine = segment(i * 256 + inside) - s1
+        u = i - begin + s1 - s0
+        o = jnp.where(
+            mine == 0,
+            parts[jnp.minimum(u, UNITS - 1)],
+            jnp.where(
+                mine == 1, parts[jnp.minimum(u + 1, UNITS - 1)], parts[jnp.minimum(u + 2, UNITS - 1)]
+            ),
+        )
         lo = jnp.concatenate([o[:128, 64:], o[:128, :64]], 1)
         out[i] = jnp.where(low, lo, o[128:]).astype(B)
         finished(i)
         return 0
 
-    lax.fori_loop(begin, end, block, 0)
+    lax.fori_loop(begin, begin + HALF, assemble, 0)
 
 
 def greet(axis):
@@ -241,98 +253,104 @@
     return me
 
 
-def slot_of(d):
-    return jnp.where(d < CHAINS, d // 2, HEADS + (d - CHAINS) // PER_HEAD)
-
-
-def with_queries(block, d):
-    third = (d - CHAINS) % PER_HEAD
-    return (d < CHAINS) | ((block >= third_begin(third)) & (block < third_begin(third + 1)))
+def device_of(place, core):
+    y, m = place // 3, place % 3
+    z = m + jnp.where(m >= y, 1, 0)
+    return (y * 4 + z) * 2 + core
+
+
+def slot_of(place):
+    return place // 2 + HEADS * (place % 2)
 
 
 def sweep_kernel(
     src, rate, ids, w1, b1, w2, b2i, gain, bias, res,
-    buf, out, W1, W2, W2b, b2, send_sem, recv_sem, own_sem, res_send, res_recv,
+    buf, out, parts, W1, W2, W2b, b2, send_sem, recv_sem, own_sem, pass_sem, res_send, res_recv,
 ):
     me = greet("tm")
+    core, y, z = me % 2, me // 8, me // 2 % 4
+    place = y * 3 + z - jnp.where(z > y, 1, 0)
+    active = y != z
+    is_chain = active & (place % 2 == 0)
+    is_attention = active & (place % 2 == 1)
+    head = place // 2
+    half = me // HALF
     short = pl.ds(0, 256)
 
-    def parcel(d, part):
-        slot = slot_of(d)
+    def parcel(r):
         return pltpu.make_async_remote_copy(
-            src_ref=src.at[slot, short] if part else src.at[slot],
-            dst_ref=buf.at[me, short] if part else buf.at[me],
-            send_sem=send_sem.at[d],
+            src_ref=src.at[slot_of(r)],
+            dst_ref=buf.at[me],
+            send_sem=send_sem.at[r],
             recv_sem=recv_sem.at[me],
-            device_id={"tm": d},
+            device_id={"tm": device_of(r, half)},
             device_id_type=MESH,
         )
 
-    def each(first, count, stride, act):
+    def each(kind, count, act):
         @pl.loop(0, count)
         def _(k):
-            d = first + stride * k
-
-            @pl.when(d != me)
+            r = 2 * k + kind
+
+            @pl.when(device_of(r, half) != me)
             def _():
-                act(d)
-
-    def start(d):
-        @pl.when(with_queries(me, d))
-        def _():
-            parcel(d, False).start()
-
-        @pl.when(jnp.logical_not(with_queries(me, d)))
-        def _():
-            parcel(d, True).start()
-
-    def sent(d):
-        @pl.when(with_queries(me, d))
-        def _():
-            parcel(d, False).wait_send()
-
-        @pl.when(jnp.logical_not(with_queries(me, d)))
-        def _():
-            parcel(d, True).wait_send()
-
-    @pl.when(me < ROLES)
+                act(r)
+
+    @pl.when(active & (core == half))
     def _():
-        own = pltpu.make_async_copy(src.at[slot_of(me)], buf.at[me], own_sem)
+        own = pltpu.make_async_copy(src.at[slot_of(place)], buf.at[me], own_sem)
         own.start()
         own.wait()
 
-    early, late = me < 8, me >= 24
-    each(jnp.where(late, 1, 0), jnp.where(early | late, HEADS, 0), 2, start)
-    each(CHAINS, PER_HEAD * HEADS, 1, start)
-    each(jnp.where(me < 16, 0, 1), jnp.where(early | late, 0, HEADS), 2, start)
-    each(jnp.where(me < 16, 1, 0), HEADS, 2, start)
-
-    def landed(i):
-        @pl.when(i != me)
-        def _():
-            @pl.when(with_queries(i, me))
-            def _():
-                pltpu.make_async_copy(buf.at[i], buf.at[i], recv_sem.at[i]).wait()
-
-            @pl.when(jnp.logical_not(with_queries(i, me)))
-            def _():
-                got = buf.at[i, short]
-                pltpu.make_async_copy(got, got, recv_sem.at[i]).wait()
-
-    slot = jnp.where(me < CHAINS, me, CHAINS + (me - CHAINS) // PER_HEAD)
+    urgent = (me < 8) | (me >= N_TM - 8)
+    each(0, jnp.where(urgent, HEADS, 0), lambda r: parcel(r).start())
+    each(1, HEADS, lambda r: parcel(r).start())
+    each(0, jnp.where(urgent, 0, HEADS), lambda r: parcel(r).start())
+
+    def passing(i, part):
+        block = buf.at[i, short] if part else buf.at[i]
+        return pltpu.make_async_remote_copy(
+            src_ref=block,
+            dst_ref=block,
+            send_sem=pass_sem.at[i],
+            recv_sem=recv_sem.at[i],
+            device_id={"tm": me + 1 - 2 * core},
+            device_id_type=MESH,
+        )
+
+    def landed(i, part):
+        direct = i // HALF == core
+
+        @pl.when(direct & (i != me))
+        def _():
+            pltpu.make_async_copy(buf.at[i], buf.at[i], recv_sem.at[i]).wait()
+
+        @pl.when(direct)
+        def _():
+            passing(i, part).start()
+
+        @pl.when(jnp.logical_not(direct))
+        def _():
+            passing(i, part).wait_recv()
+
+    def result(i):
+        slot = jnp.where(is_chain, 2 * head + core, CHAINS + head)
+        return out.at[i], res.at[slot], res_send.at[i], res_recv.at[slot]
 
     def away(i):
+        block, there, sent, got = result(i)
         return pltpu.make_async_remote_copy(
-            src_ref=out.at[i],
-            dst_ref=res.at[slot],
-            send_sem=res_send.at[i],
-            recv_sem=res_recv.at[slot],
+            src_ref=block,
+            dst_ref=there,
+            send_sem=sent,
+            recv_sem=got,
             device_id={"tm": i},
             device_id_type=MESH,
         )
 
     def here(i):
-        return pltpu.make_async_copy(out.at[i], res.at[slot], res_send.at[i])
+        block, there, sent, _ = result(i)
+        return pltpu.make_async_copy(block, there, sent)
 
     def deliver(i):
         @pl.when(i != me)
@@ -352,10 +370,12 @@
         def _():
             here(i).wait()
 
-    @pl.when(me < CHAINS)
+    def passed(part):
+        pl.loop(core * HALF, core * HALF + HALF)(lambda i: passing(i, part).wait_send())
+
+    @pl.when(is_chain)
     def _():
-        rev = me % 2 == 1
-        head = me // 2
+        rev = core == 1
         row = pl.ds(head, 1)
 
         def real(i):
@@ -363,23 +383,30 @@
 
         chain(
             rev, rate[head], buf, w1[head], b1[row, :], w2[head], b2i[row, :], gain[row, :], bias[row, :],
-            out, W1, W2, W2b, b2, lambda i: landed(real(i)), lambda i: deliver(real(i)),
-        )
+            out, W1, W2, W2b, b2, lambda i: landed(real(i), False), lambda i: deliver(real(i)),
+        )
+        passed(False)
         pl.loop(0, N_TM)(delivered)
 
-    @pl.when((me >= CHAINS) & (me < ROLES))
+    @pl.when(is_attention)
     def _():
-        third = (me - CHAINS) % PER_HEAD
-        pl.loop(0, N_TM)(landed)
-        attend(third, ids[...], buf, out, deliver)
-        pl.loop(third_begin(third), third_begin(third + 1))(delivered)
-
-    each(0, ROLES, 1, sent)
+        pl.loop(core * HALF, core * HALF + HALF)(lambda i: landed(i, True))
+        other = (1 - core) * HALF
+        pl.loop(other, other + HALF)(lambda i: landed(i, True))
+        attend(core, ids, buf, parts, out, deliver)
+        passed(True)
+        pl.loop(core * HALF, core * HALF + HALF)(delivered)
+
+    each(0, HEADS, lambda r: parcel(r).wait_send())
+    each(1, HEADS, lambda r: parcel(r).wait_send())
 
     @pl.loop(0, 3 * HEADS)
     def _(slot):
-        third = jnp.where(me < third_begin(1), 0, jnp.where(me < third_begin(2), 1, 2))
-        origin = jnp.where(slot < CHAINS, slot, CHAINS + (slot - CHAINS) * PER_HEAD + third)
+        origin = jnp.where(
+            slot < CHAINS,
+            device_of(slot // 2 * 2, slot % 2),
+            device_of((slot - CHAINS) * 2 + 1, half),
+        )
 
         @pl.when(origin != me)
         def _():
@@ -569,17 +596,19 @@
     res = call(
         sweep_kernel,
         [jax.ShapeDtypeStruct((3 * HEADS, 128, 128), B)],
-        ("vs" + "v" * 7, "h"),
+        ("vss" + "v" * 6, "h"),
         [
             pltpu.VMEM((N_TM, PACK, 128), B),
             pltpu.VMEM((N_TM, 128, 128), B),
+            pltpu.VMEM((UNITS, 256, 128), F),
             pltpu.VMEM((128, 256), F),
             pltpu.VMEM((64, 256), F),
             pltpu.VMEM((64, 256), B),
             pltpu.VMEM((1, 128), F),
-            dma((N_TM,)),
+            dma((PLACES,)),
             dma((N_TM,)),
             dma,
+            dma((N_TM,)),
             dma((N_TM,)),
             dma((3 * HEADS,)),
         ],
@@ -588,7 +617,7 @@
     )(
         src,
         inner_rate,
-        segment_ids.reshape(64, 128),
+        segment_ids,
         inner_w1,
         inner_b1,
         inner_w2,

time: 186 us -> 172 us (0.925)
  Pallas kernels: 180 us -> 168 us
    pallas_call x1, Pallas kernels: 126 us -> 115 us  [local(): call(sweep_kernel, [jax.ShapeDtypeStruct((3 * HEADS, 128, 128), B)], ('vs...]
where the time goes in v3:
time: 172 us
  Pallas kernels  168 us (98%)
  local copies, waits for them, and re-layouts  4.27 us (2%)
    pallas_call x1, Pallas kernels, local(): call(sweep_kernel, [jax.ShapeDtypeStruct((3 * HEADS, 128, 128), B)], ('vs...  115 us
    pallas_call x1, Pallas kernels, local(): call(project_kernel, [jax.ShapeDtypeStruct((2 * HEADS, PACK, 128), B), ja...  28.1 us
    pallas_call x1, Pallas kernels, local(): call(finish_kernel, [jax.ShapeDtypeStruct((rows, WIDTH), B)], ('vvvv', 'v...  25.2 us
    unnamed x22, local copies, waits for them, and re-layouts  4.27 us

profile of v3, /device:TPU:6, one launch (start us, length us, event | category | flops | bytes accessed | tf_op | source)
XLA Modules:
  0.0 172.3 jit_solution(3612163378804525661)
XLA Ops:
  0.0 1.3 copy.13.w2
  1.3 0.0 copy-start.2
  1.3 0.9 copy-done.2
  2.2 0.0 copy-start.4
  2.2 0.7 copy-done.4
  2.9 0.0 copy-start.5
  2.9 0.7 copy-done.5
  3.6 0.0 copy-start.1
  3.6 0.0 copy-start.3
  3.6 0.0 copy-start.6
  3.6 0.0 copy-start.7
  3.6 0.0 copy-start.9
  3.6 28.1 %project.1 = (bf16[12,384,128]{2,1,0:T(8,128)(2,1)S(1)}, f32[256,384]{1,0:T(8,128)S(1)}) custom-call(bf16[256,384]{1,0:T(8,128)(2,1)S(1)} %copy-done.2, bf16[3,3072,384]{2,1,0:T(8,128)(2,1)} %w_hbm.1, f32[6,64]{1,0:T(8,128)S(1)} %copy-done.4, f32[6,64]{1,0:T(8,128)S(1)} %copy-done.5), custom_call_target="tpu_custom_call" | custom-call | tf_op jit(solution)/shard_map/project/pallas_call | solution.py:578
  31.7 0.0 copy-start
  31.7 0.0 copy-start.8
  31.7 0.0 copy-done.1
  31.7 0.0 copy-done.3
  31.7 0.0 copy-done.6
  31.7 0.0 copy-done.7
  31.7 0.0 copy-done.9
  31.7 114.6 %sweep.1.res = bf16[18,128,128]{2,1,0:T(8,128)(2,1)S(1)} custom-call(bf16[12,384,128]{2,1,0:T(8,128)(2,1)S(1)} %get-tuple-element.7.src, f32[6]{0:T(128)S(1)} %copy-done.9, s32[8192]{0:T(1024)S(1)} %copy-done.3, f32[6,64,256]{2,1,0:T(8,128)S(1)} %copy-done.1, f32[6,256]{1,0:T(8,128)S(1)} %copy-done.6, f32[6,256,64]{2,1,0:T(8,128)S(1)} %copy.13.w2, ...), custom_call_target="tpu_custom_call" | custom-call | tf_op jit(solution)/shard_map/sweep/pallas_call | solution.py:596
  146.4 0.0 copy-done
  146.4 0.0 copy-done.8
  146.4 25.2 %finish.1 = bf16[256,384]{1,0:T(8,128)(2,1)S(1)} custom-call(bf16[18,128,128]{2,1,0:T(8,128)(2,1)S(1)} %sweep.1.res, f32[256,384]{1,0:T(8,128)S(1)} %get-tuple-element.8.qrows, f32[6,64]{1,0:T(8,128)S(1)} %copy-done.8, bf16[384,3072]{1,0:T(8,128)(2,1)S(1)} %copy-done), custom_call_target="tpu_custom_call" | custom-call | tf_op jit(solution)/shard_map/finish/pallas_call | solution.py:628
  171.6 0.7 copy.15
Async XLA Ops:
  1.3 0.9 copy-start.2
  2.2 0.7 copy-start.4
  2.9 0.7 copy-start.5
  3.6 28.1 %copy-start.1 = (f32[6,64,256]{2,1,0:T(8,128)S(1)}, f32[6,64,256]{2,1,0:T(8,128)}, u32[]{:S(2)}) copy-start(f32[6,64,256]{2,1,0:T(8,128)} %w1.1) | copy-start | bytes 1179652
  3.6 28.1 %copy-start.3 = (s32[8192]{0:T(1024)S(1)}, s32[8192]{0:T(1024)}, u32[]{:S(2)}) copy-start(s32[8192]{0:T(1024)} %ids.1) | copy-start | bytes 98308
  3.6 28.1 %copy-start.6 = (f32[6,256]{1,0:T(8,128)S(1)}, f32[6,256]{1,0:T(8,128)}, u32[]{:S(2)}) copy-start(f32[6,256]{1,0:T(8,128)} %b1.1) | copy-start | bytes 18436
  3.6 28.1 %copy-start.7 = (f32[6,64]{1,0:T(8,128)S(1)}, f32[6,64]{1,0:T(8,128)}, u32[]{:S(2)}) copy-start(f32[6,64]{1,0:T(8,128)} %b2i.1) | copy-start | bytes 4612
  3.6 28.2 %copy-start.9 = (f32[6]{0:T(128)S(1)}, f32[6]{0:T(128)}, u32[]{:S(2)}) copy-start(f32[6]{0:T(128)} %rate.1) | copy-start | bytes 76
  31.7 114.7 %copy-start = (bf16[384,3072]{1,0:T(8,128)(2,1)S(1)}, bf16[384,3072]{1,0:T(8,128)(2,1)}, u32[]{:S(2)}) copy-start(bf16[384,3072]{1,0:T(8,128)(2,1)} %w.1) | copy-start | bytes 7077892
  31.7 114.7 %copy-start.8 = (f32[6,64]{1,0:T(8,128)S(1)}, f32[6,64]{1,0:T(8,128)}, u32[]{:S(2)}) copy-start(f32[6,64]{1,0:T(8,128)} %gate.1) | copy-start | bytes 4612

commit v4 on v3

--- a/solution.py
+++ b/solution.py
@@ -82,7 +82,6 @@
     arrived(0)
     W1[0:64] = w1
     W1[64:128] = jnp.where(lax.broadcasted_iota(jnp.int32, (64, 256), 0) == 0, b1, 0.0)
-    w2 = w2.T
     W2[...] = w2 - jnp.mean(w2, 0, keepdims=True)
     W2b[...] = W2[...].astype(B)
     valid = lane < 64
@@ -110,33 +109,32 @@
         W2t = W2b[...]
         W2z = jnp.concatenate([W2t, zero_rows], 0)
         b2t = b2[...]
-        AW = mm(Ab[:, :64], W2t)
         R = mm(jnp.concatenate([Pt, KTs], 0), G1)
         Z1 = base - R[:64]
         W1n = W1[...] - R[64:]
         W1[...] = W1n
         W1b = W1n.astype(B)
+        Kn = augment(load_ka(t + 1))
+        Y = mm(jnp.concatenate([load_q(t - 1), Kn], 0), W1b)
+        Zq = mm(gelu(Y[:64]).astype(B), W2z, NT) + b2t
         X2, dX = gelu_both(Z1)
         X2b = X2.astype(B)
         Z = mm(X2b, W2z, NT) + b2t
         Zg = Z * g2
-        D = mm(jnp.concatenate([Zg.astype(B), Z.astype(B)], 0)[:, :64], W2t)
         mA = rowsum(A)
         S1, S2, S3, S4 = rowsum(Z * Z), rowsum(Zg), rowsum(Z * Zg), rowsum(A * Z)
         inv = lax.rsqrt(S1 + EPS)
         a1 = inv * inv
         a3 = a1 * (a1 * S3 + inv * S4)
-        G1n = ((a1 * D[:64] + inv * AW - a3 * D[64:]) * dX).astype(B)
         G2 = a1 * Zg + inv * A - a3 * Z - inv * (inv * S2 + mA)
-        U = mm(G2.astype(B)[:, :64], X2b, TN)
+        G2b = G2.astype(B)[:, :64]
+        G1n = (mm(G2b, W2t) * dX).astype(B)
+        U = mm(G2b, X2b, TN)
         W2n = W2[...] - s * U
         W2b[...] = W2n.astype(B)
         W2[...] = W2n - jnp.mean(W2n, 0, keepdims=True)
         b2n = jnp.where(valid_row, b2t - s * jnp.sum(G2, 0, keepdims=True), 0.0)
         b2[...] = jnp.where(valid_row, b2n - rowsum(b2n), 0.0)
-        Kn = augment(load_ka(t + 1))
-        Y = mm(jnp.concatenate([load_q(t - 1), Kn], 0), W1b)
-        Zq = mm(gelu(Y[:64]).astype(B), W2z, NT) + b2t
         Pn = (s * mm(Kn, Kt, NT)).astype(B)
         KTn = (s * Kt.astype(F)).T.astype(B)
         z = jnp.where(valid, Zlast - rowsum(Zlast), 0.0)
@@ -239,18 +237,18 @@
     lax.fori_loop(begin, begin + HALF, assemble, 0)
 
 
-def greet(axis):
-    me, n = lax.axis_index(axis), lax.axis_size(axis)
+def greet():
     barrier = pltpu.get_barrier_semaphore()
-
-    @pl.loop(1, n)
-    def _(k):
-        pl.semaphore_signal(
-            barrier, inc=1, device_id={axis: lax.rem(me + k, n)}, device_id_type=MESH
-        )
-
-    pl.semaphore_wait(barrier, n - 1)
-    return me
+    for axis, n in (("head", N_HEAD), ("tm", N_TM)):
+        me = lax.axis_index(axis)
+
+        @pl.loop(1, n)
+        def _(k):
+            pl.semaphore_signal(
+                barrier, inc=1, device_id={axis: lax.rem(me + k, n)}, device_id_type=MESH
+            )
+
+    pl.semaphore_wait(barrier, N_HEAD + N_TM - 2)
 
 
 def device_of(place, core):
@@ -263,11 +261,18 @@
     return place // 2 + HEADS * (place % 2)
 
 
-def sweep_kernel(
-    src, rate, ids, w1, b1, w2, b2i, gain, bias, res,
-    buf, out, parts, W1, W2, W2b, b2, send_sem, recv_sem, own_sem, pass_sem, res_send, res_recv,
+def layer_kernel(
+    tok, w_hbm, wo_hbm, rate, ids, w1, b1, w2, b2i, gain, bias, gate, final,
+    toks, w, acc, src, qrows, wo, buf, out, parts, W1, W2, W2b, b2, res, mixed, terms, got,
+    tok_send, tok_recv, w_sem, wo_sem, send_sem, recv_sem, own_sem, pass_sem, res_send, res_recv,
+    term_send, term_recv,
 ):
-    me = greet("tm")
+    fetch = pltpu.make_async_copy(w_hbm, w, w_sem)
+    fetch.start()
+    fetch_out = pltpu.make_async_copy(wo_hbm, wo, wo_sem)
+    fetch_out.start()
+    greet()
+    me = lax.axis_index("tm")
     core, y, z = me % 2, me // 8, me // 2 % 4
     place = y * 3 + z - jnp.where(z > y, 1, 0)
     active = y != z
@@ -296,16 +301,22 @@
             def _():
                 act(r)
 
+    def dispatch(kind, head_of):
+        r = 2 * head_of + kind
+
+        @pl.when(device_of(r, half) != me)
+        def _():
+            parcel(r).start()
+
+    sent_tokens = project(
+        tok, gain, bias, fetch, src, qrows, toks, w, acc, tok_send, tok_recv, dispatch
+    )
+
     @pl.when(active & (core == half))
     def _():
         own = pltpu.make_async_copy(src.at[slot_of(place)], buf.at[me], own_sem)
         own.start()
         own.wait()
-
-    urgent = (me < 8) | (me >= N_TM - 8)
-    each(0, jnp.where(urgent, HEADS, 0), lambda r: parcel(r).start())
-    each(1, HEADS, lambda r: parcel(r).start())
-    each(0, jnp.where(urgent, 0, HEADS), lambda r: parcel(r).start())
 
     def passing(i, part):
         block = buf.at[i, short] if part else buf.at[i]
@@ -397,8 +408,6 @@
         passed(True)
         pl.loop(core * HALF, core * HALF + HALF)(delivered)
 
-    each(0, HEADS, lambda r: parcel(r).wait_send())
-    each(1, HEADS, lambda r: parcel(r).wait_send())
 
     @pl.loop(0, 3 * HEADS)
     def _(slot):
@@ -412,6 +421,12 @@
         def _():
             pltpu.make_async_copy(res.at[slot], res.at[slot], res_recv.at[slot]).wait()
 
+    fetch_out.wait()
+    finish(res, qrows, gate, wo, final, mixed, terms, got, term_send, term_recv)
+    each(0, HEADS, lambda r: parcel(r).wait_send())
+    each(1, HEADS, lambda r: parcel(r).wait_send())
+    sent_tokens()
+
 
 def tile_row(ref, g):
     return jnp.concatenate([ref[2 * g : 2 * g + 1, :], ref[2 * g + 1 : 2 * g + 2, :]], 1)
@@ -421,11 +436,8 @@
     return jnp.concatenate([x[:, 64:], x[:, :64]], 1)
 
 
-def project_kernel(tok, w_hbm, gain, bias, src, qrows, toks, w, acc, send_sem, recv_sem, w_sem):
+def project(tok, gain, bias, fetch, src, qrows, toks, w, acc, send_sem, recv_sem, dispatch):
     me = lax.axis_index("head")
-    fetch = pltpu.make_async_copy(w_hbm, w, w_sem)
-    fetch.start()
-    greet("head")
 
     def parcel(k):
         return pltpu.make_async_remote_copy(
@@ -475,25 +487,32 @@
         odd = [jnp.where(low[:64], y[a : a + 64], x[a + 64 : a + 128]) for a in (0, 128)]
         return jnp.concatenate(even, 0), jnp.concatenate(odd, 0)
 
+    def pack(g, left, right, quer, kind):
+        tops, tails = pack_rows(left, right), pack_pairs(quer)
+        for e in range(2):
+            slot = HEADS * kind + 2 * g + e
+            src[slot, 0:256, :] = tops[e].astype(B)
+            src[slot, 256:PACK, :] = tails[e].astype(B)
+            dispatch(kind, 2 * g + e)
+
+    def raw(g):
+        return (
+            acc[:, c * WIDTH + g * 128 : c * WIDTH + (g + 1) * 128].astype(B).astype(F) for c in range(3)
+        )
+
     for g in range(HEADS // 2):
-        q, k, v = (
-            acc[:, c * WIDTH + g * 128 : c * WIDTH + (g + 1) * 128].astype(B).astype(F) for c in range(3)
-        )
-        qn, kn, vn = scaled(q), scaled(k), scaled(v)
+        qn, kn, vn = (scaled(x) for x in raw(g))
         qrows[:, g * 128 : (g + 1) * 128] = qn
-        aim = (tile_row(bias, g) - (vn - kn)) * tile_row(gain, g)
-        sets = ((kn, aim, qn, 0), (k, v, q * HDIM**-0.5, HEADS))
-        for left, right, quer, offset in sets:
-            tops, tails = pack_rows(left, right), pack_pairs(quer)
-            for e in range(2):
-                src[offset + 2 * g + e, 0:256, :] = tops[e].astype(B)
-                src[offset + 2 * g + e, 256:PACK, :] = tails[e].astype(B)
-
-    pl.loop(1, N_HEAD)(lambda k: parcel(k).wait_send())
-
-
-def finish_kernel(res, qrows, gate, w, out, mixed, terms, got, send_sem, recv_sem):
-    me = greet("head")
+        pack(g, kn, (tile_row(bias, g) - (vn - kn)) * tile_row(gain, g), qn, 0)
+    for g in range(HEADS // 2):
+        q, k, v = raw(g)
+        pack(g, k, v, q * HDIM**-0.5, 1)
+
+    return lambda: pl.loop(1, N_HEAD)(lambda k: parcel(k).wait_send())
+
+
+def finish(res, qrows, gate, w, out, mixed, terms, got, send_sem, recv_sem):
+    me = lax.axis_index("head")
     low = lanes((64, 128)) < 64
     for g in range(HEADS // 2):
         weight = jnp.tanh(tile_row(gate, g))
@@ -541,24 +560,6 @@
     pl.loop(1, N_HEAD)(lambda k: parcel(k).wait_send())
 
 
-def call(kernel, shapes, memory, scratch, name, collective_id):
-    several = len(shapes) > 1
-    spaces = {"v": pltpu.VMEM, "s": pltpu.SMEM, "h": pl.ANY}
-    ins, outs = memory
-    specs = [pl.BlockSpec(memory_space=spaces[m]) for m in outs]
-    return pl.pallas_call(
-        kernel,
-        out_shape=shapes if several else shapes[0],
-        in_specs=[pl.BlockSpec(memory_space=spaces[m]) for m in ins],
-        out_specs=specs if several else specs[0],
-        scratch_shapes=scratch,
-        compiler_params=pltpu.CompilerParams(
-            collective_id=collective_id, has_side_effects=True, vmem_limit_bytes=48 * 2**20
-        ),
-        name=name,
-    )
-
-
 def local(
     tokens,
     qkv_weight,
@@ -575,29 +576,19 @@
 ):
     rows = tokens.shape[0]
     dma = pltpu.SemaphoreType.DMA
-    src, qrows = call(
-        project_kernel,
-        [
-            jax.ShapeDtypeStruct((2 * HEADS, PACK, 128), B),
-            jax.ShapeDtypeStruct((rows, WIDTH), F),
-        ],
-        ("vhvv", "vv"),
-        [
+    vm, sm, hbm = (pl.BlockSpec(memory_space=m) for m in (pltpu.VMEM, pltpu.SMEM, pl.ANY))
+    return pl.pallas_call(
+        layer_kernel,
+        out_shape=jax.ShapeDtypeStruct((rows, WIDTH), B),
+        in_specs=[vm, hbm, hbm, sm, sm] + [vm] * 7,
+        out_specs=vm,
+        scratch_shapes=[
             pltpu.VMEM((N_HEAD, rows, WIDTH), B),
             pltpu.VMEM(qkv_weight.shape, B),
             pltpu.VMEM((rows, 3 * WIDTH), F),
-            dma((N_HEAD,)),
-            dma((N_HEAD,)),
-            dma,
-        ],
-        "project",
-        1,
-    )(tokens, qkv_weight, norm_gain, norm_bias)
-    res = call(
-        sweep_kernel,
-        [jax.ShapeDtypeStruct((3 * HEADS, 128, 128), B)],
-        ("vss" + "v" * 6, "h"),
-        [
+            pltpu.VMEM((2 * HEADS, PACK, 128), B),
+            pltpu.VMEM((rows, WIDTH), F),
+            pltpu.VMEM(out_weight.shape, B),
             pltpu.VMEM((N_TM, PACK, 128), B),
             pltpu.VMEM((N_TM, 128, 128), B),
             pltpu.VMEM((UNITS, 256, 128), F),
@@ -605,40 +596,41 @@
             pltpu.VMEM((64, 256), F),
             pltpu.VMEM((64, 256), B),
             pltpu.VMEM((1, 128), F),
+            pltpu.VMEM((3 * HEADS, 128, 128), B),
+            pltpu.VMEM((rows, WIDTH), B),
+            pltpu.VMEM((N_HEAD, rows, WIDTH), B),
+            pltpu.VMEM((N_HEAD, rows, WIDTH), B),
+            dma((N_HEAD,)),
+            dma((N_HEAD,)),
+            dma,
+            dma,
             dma((PLACES,)),
             dma((N_TM,)),
             dma,
             dma((N_TM,)),
             dma((N_TM,)),
             dma((3 * HEADS,)),
+            dma((N_HEAD,)),
+            dma((N_HEAD,)),
         ],
-        "sweep",
-        2,
+        compiler_params=pltpu.CompilerParams(
+            collective_id=1, has_side_effects=True, vmem_limit_bytes=56 * 2**20
+        ),
+        name="layer",
     )(
-        src,
+        tokens,
+        qkv_weight,
+        out_weight,
         inner_rate,
         segment_ids,
         inner_w1,
         inner_b1,
-        inner_w2,
+        jnp.swapaxes(inner_w2, 1, 2),
         inner_b2,
         norm_gain,
         norm_bias,
+        out_gate,
     )
-    return call(
-        finish_kernel,
-        [jax.ShapeDtypeStruct((rows, WIDTH), B)],
-        ("vvvv", "v"),
-        [
-            pltpu.VMEM((rows, WIDTH), B),
-            pltpu.VMEM((N_HEAD, rows, WIDTH), B),
-            pltpu.VMEM((N_HEAD, rows, WIDTH), B),
-            dma((N_HEAD,)),
-            dma((N_HEAD,)),
-        ],
-        "finish",
-        3,
-    )(res, qrows, out_gate, out_weight)
 
 
 def solution(mesh):

time: 172 us -> 168 us (0.977)
  local copies, waits for them, and re-layouts: 4.27 us -> 1.62 us
  Pallas kernels: 168 us -> 166 us
    unnamed x22 -> x1, local copies, waits for them, and re-layouts: 4.27 us -> 1.62 us
    pallas_call x3 -> x1, Pallas kernels: 168 us -> 166 us  [local(): pl.pallas_call(layer_kernel, out_shape=jax.ShapeDtypeStruct((rows, WIDTH)...]
where the time goes in v4:
time: 168 us
  Pallas kernels  166 us (99%)
    pallas_call x1, Pallas kernels, local(): pl.pallas_call(layer_kernel, out_shape=jax.ShapeDtypeStruct((rows, WIDTH)...  166 us

profile of v4, /device:TPU:6, one launch (start us, length us, event | category | flops | bytes accessed | tf_op | source)
XLA Modules:
  0.0 168.0 jit_solution(16898460680222533777)
XLA Ops:
  0.0 166.3 %layer.1 = bf16[256,384]{1,0:T(8,128)(2,1)} custom-call(bf16[256,384]{1,0:T(8,128)(2,1)} %tok.1, bf16[3,3072,384]{2,1,0:T(8,128)(2,1)} %w_hbm.1, bf16[384,3072]{1,0:T(8,128)(2,1)} %wo_hbm.1, f32[6]{0:T(128)} %rate.1, s32[8192]{0:T(1024)} %ids.1, f32[6,64,256]{2,1,0:T(8,128)} %w1.1, f32[6,256]{1,0:T(8,128)} %b1.1, f32[6,64,256]{2,1,0:T(8,128)} %bitcast.1, ...), custom_call_target="tpu_custom_call" | custom-call | tf_op jit(solution)/shard_map/layer/pallas_call | solution.py:580
  166.3 1.6 copy.14

commit v5 on v4

--- a/solution.py
+++ b/solution.py
@@ -121,18 +121,18 @@
         X2b = X2.astype(B)
         Z = mm(X2b, W2z, NT) + b2t
         Zg = Z * g2
-        mA = rowsum(A)
-        S1, S2, S3, S4 = rowsum(Z * Z), rowsum(Zg), rowsum(Z * Zg), rowsum(A * Z)
+        S1, S3, S4 = rowsum(Z * Z), rowsum(Z * Zg), rowsum(A * Z)
         inv = lax.rsqrt(S1 + EPS)
         a1 = inv * inv
         a3 = a1 * (a1 * S3 + inv * S4)
-        G2 = a1 * Zg + inv * A - a3 * Z - inv * (inv * S2 + mA)
+        G2 = a1 * Zg + inv * A - a3 * Z
         G2b = G2.astype(B)[:, :64]
         G1n = (mm(G2b, W2t) * dX).astype(B)
         U = mm(G2b, X2b, TN)
         W2n = W2[...] - s * U
+        W2n = W2n - jnp.mean(W2n, 0, keepdims=True)
         W2b[...] = W2n.astype(B)
-        W2[...] = W2n - jnp.mean(W2n, 0, keepdims=True)
+        W2[...] = W2n
         b2n = jnp.where(valid_row, b2t - s * jnp.sum(G2, 0, keepdims=True), 0.0)
         b2[...] = jnp.where(valid_row, b2n - rowsum(b2n), 0.0)
         Pn = (s * mm(Kn, Kt, NT)).astype(B)
@@ -439,19 +439,6 @@
 def project(tok, gain, bias, fetch, src, qrows, toks, w, acc, send_sem, recv_sem, dispatch):
     me = lax.axis_index("head")
 
-    def parcel(k):
-        return pltpu.make_async_remote_copy(
-            src_ref=tok,
-            dst_ref=toks.at[me],
-            send_sem=send_sem.at[k],
-            recv_sem=recv_sem.at[me],
-            device_id={"head": lax.rem(me + k, N_HEAD)},
-            device_id_type=MESH,
-        )
-
-    pl.loop(1, N_HEAD)(lambda k: parcel(k).start())
-    fetch.wait()
-
     def add(x, s, fresh):
         rows = pl.ds(pl.multiple_of(s * WIDTH, WIDTH), WIDTH)
         for c in range(3):
@@ -459,23 +446,64 @@
             y = mm(x, w[c, rows, :])
             acc[:, cols] = y if fresh else acc[:, cols] + y
 
+    level, x = me // 4, me % 4
+
+    def at(other, step):
+        z = 1 - level if other else level
+        return z * 4 + (x + step) % 4
+
+    right, left, across = at(0, 1), at(0, 3), at(1, 0)
+    sends = []
+
+    def push(block, s, dest, part=None):
+        rows = pl.ds(0, 256) if part is None else pl.ds(128 * part, 128)
+        copy = pltpu.make_async_remote_copy(
+            src_ref=block.at[rows],
+            dst_ref=toks.at[s, rows],
+            send_sem=send_sem.at[len(sends)],
+            recv_sem=recv_sem.at[s, part or 0],
+            device_id={"head": dest},
+            device_id_type=MESH,
+        )
+        copy.start()
+        sends.append(copy)
+
+    def take(s, halves=False):
+        for part in range(2 if halves else 1):
+            rows = pl.ds(128 * part, 128) if halves else pl.ds(0, 256)
+            piece = toks.at[s, rows]
+            pltpu.make_async_copy(piece, piece, recv_sem.at[s, part]).wait()
+
+    for dest in (across, right, left):
+        push(tok, me, dest)
+    fetch.wait()
     add(tok[...], me, True)
-
-    @pl.loop(1, N_HEAD)
-    def _(k):
-        s = lax.rem(me + N_HEAD - k, N_HEAD)
-        pltpu.make_async_copy(toks.at[s], toks.at[s], recv_sem.at[s]).wait()
-        add(toks[s], s, False)
+    take(across)
+    push(toks.at[across], across, right)
+    push(toks.at[across], across, left)
+    for other in (0, 1):
+        for step, dest, part in ((3, right, 0), (1, left, 1)):
+            s = at(other, step)
+            take(s)
+            push(toks.at[s], s, dest, part)
+            if not other and step == 3:
+                add(toks[across], across, False)
+            add(toks[s], s, False)
+    for other in (0, 1):
+        take(at(other, 2), True)
+        add(toks[at(other, 2)], at(other, 2), False)
 
     low = lanes((256, 128)) < 64
     low_half = lanes((128, 128)) < 64
     r = lax.broadcasted_iota(jnp.int32, (128, 128), 0)
     same = jnp.where((r < 64) == low_half, 1.0 / HDIM, 0.0).astype(B)
 
+    def group_mean(x):
+        hi = x.astype(B)
+        return mm(hi, same) + mm((x - hi.astype(F)).astype(B), same)
+
     def scaled(x):
-        sq = x * x
-        hi = sq.astype(B)
-        return x * lax.rsqrt(mm(hi, same) + mm((sq - hi.astype(F)).astype(B), same) + EPS)
+        return x * lax.rsqrt(group_mean(x * x) + EPS)
 
     def pack_rows(left, right):
         pairs = [jnp.where(low, left, swap_halves(right)), jnp.where(low, swap_halves(left), right)]
@@ -503,12 +531,17 @@
     for g in range(HEADS // 2):
         qn, kn, vn = (scaled(x) for x in raw(g))
         qrows[:, g * 128 : (g + 1) * 128] = qn
-        pack(g, kn, (tile_row(bias, g) - (vn - kn)) * tile_row(gain, g), qn, 0)
+        aim = (tile_row(bias, g) - (vn - kn)) * tile_row(gain, g)
+        pack(g, kn, aim - group_mean(aim), qn, 0)
     for g in range(HEADS // 2):
         q, k, v = raw(g)
         pack(g, k, v, q * HDIM**-0.5, 1)
 
-    return lambda: pl.loop(1, N_HEAD)(lambda k: parcel(k).wait_send())
+    def sent():
+        for copy in sends:
+            copy.wait_send()
+
+    return sent
 
 
 def finish(res, qrows, gate, w, out, mixed, terms, got, send_sem, recv_sem):
@@ -600,8 +633,8 @@
             pltpu.VMEM((rows, WIDTH), B),
             pltpu.VMEM((N_HEAD, rows, WIDTH), B),
             pltpu.VMEM((N_HEAD, rows, WIDTH), B),
-            dma((N_HEAD,)),
-            dma((N_HEAD,)),
+            dma((9,)),
+            dma((N_HEAD, 2)),
             dma,
             dma,
             dma((PLACES,)),

time: 168 us -> 163 us (0.970); the launches traced: 168 us -> 161 us
  Pallas kernels: 166 us -> 159 us
    pallas_call x1, Pallas kernels: 166 us -> 159 us  [local(): pl.pallas_call(layer_kernel, out_shape=jax.ShapeDtypeStruct((rows, WIDTH)...]
where the time goes in v5:
time: 163 us; the launch traced here: 161 us
  Pallas kernels  159 us (98%)
    pallas_call x1, Pallas kernels, local(): pl.pallas_call(layer_kernel, out_shape=jax.ShapeDtypeStruct((rows, WIDTH)...  159 us

profile of v5, /device:TPU:6, one launch (start us, length us, event | category | flops | bytes accessed | tf_op | source)
XLA Modules:
  0.0 160.8 jit_solution(17061862518986068809)
XLA Ops:
  0.0 159.2 %layer.1 = bf16[256,384]{1,0:T(8,128)(2,1)} custom-call(bf16[256,384]{1,0:T(8,128)(2,1)} %tok.1, bf16[3,3072,384]{2,1,0:T(8,128)(2,1)} %w_hbm.1, bf16[384,3072]{1,0:T(8,128)(2,1)} %wo_hbm.1, f32[6]{0:T(128)} %rate.1, s32[8192]{0:T(1024)} %ids.1, f32[6,64,256]{2,1,0:T(8,128)} %w1.1, f32[6,256]{1,0:T(8,128)} %b1.1, f32[6,64,256]{2,1,0:T(8,128)} %bitcast.1, ...), custom_call_target="tpu_custom_call" | custom-call | tf_op jit(solution)/shard_map/layer/pallas_call | solution.py:613
  159.2 1.6 %copy.14 = bf16[256,384]{1,0:T(8,128)(2,1)} copy(bf16[256,384]{1,0:T(8,128)(2,1)} %layer.1) | data formatting | bytes 393216

commit v6 on v5

--- a/solution.py
+++ b/solution.py
@@ -569,28 +569,59 @@
         cols = pl.ds(pl.multiple_of(d * WIDTH, WIDTH), WIDTH)
         return mm(mixed[...], w[:, cols])
 
-    def parcel(k):
-        return pltpu.make_async_remote_copy(
-            src_ref=terms.at[k],
-            dst_ref=got.at[me],
-            send_sem=send_sem.at[k],
-            recv_sem=recv_sem.at[me],
-            device_id={"head": lax.rem(me + k, N_HEAD)},
+    level, x = me // 4, me % 4
+
+    def at(other, step):
+        z = 1 - level if other else level
+        return z * 4 + (x + step) % 4
+
+    right, left, across = at(0, 1), at(0, 3), at(1, 0)
+    first, second = pl.ds(0, 128), pl.ds(128, 128)
+    sends = []
+
+    def push(block, there, sem, dest):
+        copy = pltpu.make_async_remote_copy(
+            src_ref=block,
+            dst_ref=there,
+            send_sem=send_sem.at[len(sends)],
+            recv_sem=recv_sem.at[sem],
+            device_id={"head": dest},
             device_id_type=MESH,
         )
-
-    @pl.loop(1, N_HEAD)
-    def _(k):
-        terms[k] = part(lax.rem(me + k, N_HEAD)).astype(B)
-        parcel(k).start()
-
-    def gather(k, total):
-        s = lax.rem(me + N_HEAD - k, N_HEAD)
-        pltpu.make_async_copy(got.at[s], got.at[s], recv_sem.at[s]).wait()
-        return total + got[s].astype(F)
-
-    out[...] = lax.fori_loop(1, N_HEAD, gather, part(me)).astype(B)
-    pl.loop(1, N_HEAD)(lambda k: parcel(k).wait_send())
+        copy.start()
+        sends.append(copy)
+
+    def take(block, sem):
+        pltpu.make_async_copy(block, block, recv_sem.at[sem]).wait()
+
+    for o in (1, 0):
+        terms[o] = part(at(o, 2)).astype(B)
+        push(terms.at[o, first], got.at[o, first], 2 * o, right)
+        push(terms.at[o, second], got.at[o, second], 2 * o + 1, left)
+    for o in (1, 0):
+        mine = part(at(o, 1))
+        take(got.at[o, first], 2 * o)
+        terms[2 + o, 0:128] = (mine[:128] + got[o, 0:128].astype(F)).astype(B)
+        terms[2 + o, 128:256] = mine[128:].astype(B)
+        push(terms.at[2 + o], got.at[2 + o], 4 + 2 * o, right)
+        mine = part(at(o, 3))
+        take(got.at[o, second], 2 * o + 1)
+        terms[4 + o, 0:128] = mine[:128].astype(B)
+        terms[4 + o, 128:256] = (mine[128:] + got[o, 128:256].astype(F)).astype(B)
+        push(terms.at[4 + o], got.at[4 + o], 5 + 2 * o, left)
+    total = {}
+    for o in (1, 0):
+        mine = part(at(o, 0))
+        take(got.at[2 + o], 4 + 2 * o)
+        take(got.at[4 + o], 5 + 2 * o)
+        total[o] = mine + got[2 + o].astype(F) + got[4 + o].astype(F)
+        if o == 1:
+            terms[6] = total[1].astype(B)
+            push(terms.at[6], got.at[6], 8, across)
+    take(got.at[6], 8)
+    out[...] = (total[0] + got[6].astype(F)).astype(B)
+    for copy in sends:
+        copy.wait_send()
 
 
 def local(
@@ -643,8 +674,8 @@
             dma((N_TM,)),
             dma((N_TM,)),
             dma((3 * HEADS,)),
-            dma((N_HEAD,)),
-            dma((N_HEAD,)),
+            dma((9,)),
+            dma((9,)),
         ],
         compiler_params=pltpu.CompilerParams(
             collective_id=1, has_side_effects=True, vmem_limit_bytes=56 * 2**20

time: 163 us -> 158 us (0.969)
  Pallas kernels: 159 us -> 154 us
    pallas_call x1, Pallas kernels: 159 us -> 154 us  [local(): pl.pallas_call(layer_kernel, out_shape=jax.ShapeDtypeStruct((rows, WIDTH)...]
where the time goes in v6:
time: 158 us; the launch traced here: 156 us
  Pallas kernels  154 us (97%)
  local copies, waits for them, and re-layouts  1.62 us (1%)
    pallas_call x1, Pallas kernels, local(): pl.pallas_call(layer_kernel, out_shape=jax.ShapeDtypeStruct((rows, WIDTH)...  154 us

profile of v6, /device:TPU:6, one launch (start us, length us, event | category | flops | bytes accessed | tf_op | source)
XLA Modules:
  0.0 155.6 jit_solution(3600405398519437312)
XLA Ops:
  0.0 154.0 %layer.1 = bf16[256,384]{1,0:T(8,128)(2,1)} custom-call(bf16[256,384]{1,0:T(8,128)(2,1)} %tok.1, bf16[3,3072,384]{2,1,0:T(8,128)(2,1)} %w_hbm.1, bf16[384,3072]{1,0:T(8,128)(2,1)} %wo_hbm.1, f32[6]{0:T(128)} %rate.1, s32[8192]{0:T(1024)} %ids.1, f32[6,64,256]{2,1,0:T(8,128)} %w1.1, f32[6,256]{1,0:T(8,128)} %b1.1, f32[6,64,256]{2,1,0:T(8,128)} %bitcast.1, ...), custom_call_target="tpu_custom_call" | custom-call | tf_op jit(solution)/shard_map/layer/pallas_call | solution.py:644
  154.0 1.6 %copy.14 = bf16[256,384]{1,0:T(8,128)(2,1)} copy(bf16[256,384]{1,0:T(8,128)(2,1)} %layer.1) | data formatting | bytes 393216

commit v7 on v6

--- a/solution.py
+++ b/solution.py
@@ -486,9 +486,11 @@
             s = at(other, step)
             take(s)
             push(toks.at[s], s, dest, part)
-            if not other and step == 3:
-                add(toks[across], across, False)
-            add(toks[s], s, False)
+        if not other:
+            add(toks[across], across, False)
+    for other in (0, 1):
+        for step in (3, 1):
+            add(toks[at(other, step)], at(other, step), False)
     for other in (0, 1):
         take(at(other, 2), True)
         add(toks[at(other, 2)], at(other, 2), False)

time: 158 us -> 158 us (level)
  no operation moved by 1% of the time
where the time goes in v7:
time: 158 us; the launch traced here: 156 us
  Pallas kernels  154 us (97%)
  local copies, waits for them, and re-layouts  1.62 us (1%)
    pallas_call x1, Pallas kernels, local(): pl.pallas_call(layer_kernel, out_shape=jax.ShapeDtypeStruct((rows, WIDTH)...  154 us

profile of v7, /device:TPU:6, one launch (start us, length us, event | category | flops | bytes accessed | tf_op | source)
XLA Modules:
  0.0 155.6 jit_solution(2007016538683898108)
XLA Ops:
  0.0 153.9 %layer.1 = bf16[256,384]{1,0:T(8,128)(2,1)} custom-call(bf16[256,384]{1,0:T(8,128)(2,1)} %tok.1, bf16[3,3072,384]{2,1,0:T(8,128)(2,1)} %w_hbm.1, bf16[384,3072]{1,0:T(8,128)(2,1)} %wo_hbm.1, f32[6]{0:T(128)} %rate.1, s32[8192]{0:T(1024)} %ids.1, f32[6,64,256]{2,1,0:T(8,128)} %w1.1, f32[6,256]{1,0:T(8,128)} %b1.1, f32[6,64,256]{2,1,0:T(8,128)} %bitcast.1, ...), custom_call_target="tpu_custom_call" | custom-call | tf_op jit(solution)/shard_map/layer/pallas_call | solution.py:646
  154.0 1.6 %copy.14 = bf16[256,384]{1,0:T(8,128)(2,1)} copy(bf16[256,384]{1,0:T(8,128)(2,1)} %layer.1) | data formatting | bytes 393216
